TPU v7x, 128 devices: a whole 4x4x4 slice. The times are simulated.
128 devices in a mesh: branch: 16 (over y, z), leaf: 8 (over x, core).
Axes of the slice: x: 4, y: 4, z: 4, core: 2. Of those that a mesh axis runs over, the one named last changes fastest.
Arguments:
- points_rhs: bfloat16 [16, 524288], P(None, ('branch', 'leaf')), may hold values from -6 to 6
- order: int32 [524288], P(('branch', 'leaf')), may hold values from 0 to 524287, as said below
- leaf_parent: int32 [2048], P(('branch', 'leaf')), may hold values from 0 to 1023, as said below
- near_list: int32 [2048, 6], P(('branch', 'leaf')), may hold values from 0 to 2047, as said below
- near_count: int32 [2048], P(('branch', 'leaf')), may hold values from 2 to 6, as said below
- far_list: int32 [1024, 4], P(('branch', 'leaf')), may hold values from 0 to 1023, as said below
- pair_mask2: int32 [128, 8], P(('branch', 'leaf')), may hold values 0 or 1
- pair_mask3: int32 [16, 16], P('branch'), may hold values 0 or 1
- basis: bfloat16 [2048, 256, 64], P(('branch', 'leaf')), may hold values from -0.375 to 0.375
- transfer1: float32 [2048, 64, 64], P(('branch', 'leaf')), may hold values from -0.5 to 0.5
- transfer2: float32 [1024, 64, 64], P(('branch', 'leaf')), may hold values from -0.25 to 0.25
- transfer3: float32 [128, 64, 64], P(('branch', 'leaf')), may hold values from -0.25 to 0.25
- couple1: float32 [1024, 4, 64, 64], P(('branch', 'leaf')), may hold values from -0.375 to 0.375
- couple2: float32 [128, 8, 64, 64], P(('branch', 'leaf')), may hold values from -0.25 to 0.25
- couple3: float32 [16, 16, 64, 64], P('branch'), may hold values from -0.1875 to 0.1875
- near_tiles: bfloat16 [2048, 6, 256, 256], P(('branch', 'leaf')), may hold values from -0.15625 to 0.15625
Outputs:
- product: bfloat16 [16, 524288], P(None, ('branch', 'leaf'))
Inputs may be any that keep to these rules, and one draw needn't show every extreme that they name: `order`: A permutation of the positions that keeps each block of 4096 positions of one device within that block. `leaf_parent`: leaf g's parent lies among the 8 clusters of the same device, g // 16 * 8 onwards; every cluster has exactly two leaves. `near_list`: row g holds distinct leaves (g + o) mod 2048 with |o| <= 8; slot 0 is g itself, slot 1 has o = -8, slot 2 has o = 8. Only the first near_count[g] slots of row g are used. `far_list`: row c holds distinct clusters (c + o) mod 1024 with 0 < |o| <= 8; slot 0 has o = 8, slot 1 has o = -8.
All inputs are finite; a program needn't handle non-finite values. No bound on the sum of `pair_mask2` or of `pair_mask3` on one device may be relied on, other than what follows from the above.
Results may differ from a plain program's by a relative error of at most 0.0034.
Values may be sent and summed in bfloat16 or wider, within the bound.
A program may use at most 64 MiB of HBM per device.

v0:
```python
import jax
import jax.numpy as jnp
from jax import lax
from jax.sharding import PartitionSpec as P

HIGH = lax.Precision.HIGHEST


def with_halo(block, sides, width):
    for axis, dim in sides:
        count = lax.axis_size(axis)
        forward = [(i, i + 1) for i in range(count - 1)]
        forward.append((count - 1, 0))
        backward = [(target, source) for source, target in forward]
        low = lax.ppermute(
            lax.slice_in_dim(block, block.shape[dim] - width, None, axis=dim), axis, forward
        )
        high = lax.ppermute(lax.slice_in_dim(block, 0, width, axis=dim), axis, backward)
        block = jnp.concatenate([low, block, high], axis=dim)
    return block


def body(
    points_rhs,
    order,
    leaf_parent,
    near_list,
    near_count,
    far_list,
    pair_mask2,
    pair_mask3,
    basis,
    transfer1,
    transfer2,
    transfer3,
    couple1,
    couple2,
    couple3,
    near_tiles,
):
    rhs_count, point_count = points_rhs.shape
    leaf_count, point_size, rank_size = basis.shape
    cluster_count = transfer2.shape[0]
    slot_count = near_tiles.shape[1]
    device_total = lax.axis_size(("branch", "leaf"))
    device = lax.axis_index(("branch", "leaf"))
    total_leaves = leaf_count * device_total
    total_clusters = cluster_count * device_total
    local_order = order % point_count
    sorted_rhs = points_rhs[:, local_order]
    leaf_rhs = sorted_rhs.reshape(rhs_count, leaf_count, point_size)
    leaf_coef = jnp.einsum("rgp,gpk->grk", leaf_rhs, basis, preferred_element_type=jnp.float32)
    moved = jnp.einsum("grk,gkl->grl", leaf_coef, transfer1, precision=HIGH)
    parent_local = leaf_parent % cluster_count
    onehot = (parent_local[:, None] == jnp.arange(cluster_count)[None, :]).astype(jnp.float32)
    cluster_coef = jnp.einsum("gc,grl->crl", onehot, moved, precision=HIGH)
    device_coef = jnp.einsum("crk,ckl->rl", cluster_coef, transfer2, precision=HIGH)[None]
    raised = jnp.einsum("drk,dkl->drl", device_coef, transfer3, precision=HIGH)
    group_coef, group_raised = (
        lax.all_gather(device_coef, "leaf", axis=0, tiled=True),
        lax.all_gather(raised, "leaf", axis=0, tiled=True),
    )
    own_root = jnp.sum(group_raised, axis=0, keepdims=True)
    subtree_coef = lax.all_gather(own_root, "branch", axis=0, tiled=True)
    top_field = jnp.einsum(
        "bj,jrk,bjkl->rl", pair_mask3.astype(jnp.float32), subtree_coef, couple3, precision=HIGH
    )
    device_field = jnp.einsum(
        "dj,jrk,djkl->rl", pair_mask2.astype(jnp.float32), group_coef, couple2, precision=HIGH
    )
    device_field = device_field + jnp.einsum("rl,kl->rk", top_field, transfer3[0], precision=HIGH)
    outer_coef = with_halo(cluster_coef, ((("branch", "leaf"), 0),), cluster_count)
    far_index = (far_list - (device - 1) * cluster_count) % total_clusters
    cluster_field = jnp.einsum("csrk,cskl->crl", outer_coef[far_index], couple1, precision=HIGH)
    cluster_field = cluster_field + jnp.einsum(
        "rl,ckl->crk", device_field, transfer2, precision=HIGH
    )
    parent_field = jnp.einsum("gc,crl->grl", onehot, cluster_field, precision=HIGH)
    leaf_field = jnp.einsum("grl,gkl->grk", parent_field, transfer1, precision=HIGH).astype(
        jnp.bfloat16
    )
    far_part = jnp.einsum("grk,gpk->rgp", leaf_field, basis, preferred_element_type=jnp.float32)
    widened = with_halo(sorted_rhs, ((("branch", "leaf"), 1),), point_count)
    window = widened.reshape(rhs_count, leaf_count + 2 * leaf_count, point_size)
    near_index = (near_list - device * leaf_count + leaf_count) % total_leaves
    usable = (jnp.arange(slot_count)[None, :] < near_count[:, None]).astype(jnp.bfloat16)
    picked = window[:, near_index] * usable[None, :, :, None]
    near_part = jnp.einsum("rgsq,gsqp->rgp", picked, near_tiles, preferred_element_type=jnp.float32)
    leaf_out = (far_part + near_part).reshape(rhs_count, point_count).astype(jnp.bfloat16)
    return jnp.zeros_like(points_rhs).at[:, local_order].set(leaf_out)


def solution(mesh):
    return jax.shard_map(
        body,
        mesh=mesh,
        in_specs=(
            P(None, ("branch", "leaf")),
            P(("branch", "leaf")),
            P(("branch", "leaf")),
            P(("branch", "leaf"), None),
            P(("branch", "leaf")),
            P(("branch", "leaf"), None),
            P(("branch", "leaf"), None),
            P("branch", None),
            P(("branch", "leaf"), None, None),
            P(("branch", "leaf"), None, None),
            P(("branch", "leaf"), None, None),
            P(("branch", "leaf"), None, None),
            P(("branch", "leaf"), None, None, None),
            P(("branch", "leaf"), None, None, None),
            P("branch", None, None, None),
            P(("branch", "leaf"), None, None, None),
        ),
        out_specs=P(None, ("branch", "leaf")),
        check_vma=False,
    )
```

profile of v0, /device:TPU:8, one launch (start us, length us, event | category | flops | bytes accessed | tf_op | source)
XLA Modules:
  0.0 115.5 jit_solution(9925135717326897531)
XLA Ops:
  0.0 0.0 copy-start
  0.0 0.8 broadcast_clamp_fusion
  0.8 1.4 %copy.63 = bf16[16,4096]{0,1:T(8,128)(2,1)S(1)} copy(bf16[16,4096]{1,0:T(8,128)(2,1)} %param.16) | data formatting | bytes 262144 | tf_op args[0]
  2.2 0.7 and_select_fusion
  2.9 12.1 %gather_fusion = bf16[4096,16]{1,0:T(8,128)(2,1)S(1)} fusion(bf16[16,4096]{0,1:T(8,128)(2,1)S(1)} %copy.63, s32[4096]{0:T(1024)S(1)} %get-tuple-element.5), kind=kCustom, calls=%fused_computation | custom fusion | bytes 278528 | tf_op jit(solution)/shard_map/gather | solution.py:50
  15.0 1.5 %fusion.34 = f32[16,16,64]{2,1,0:T(8,128)S(1)} fusion(bf16[16,16,256]{0,2,1:T(8,128)(2,1)S(1)} %bitcast.74, bf16[16,256,64]{1,2,0:T(8,128)(2,1)} %param.24), kind=kOutput, calls=%fused_computation.70 | convolution fusion | flops 8388608 | bytes 720896 | tf_op jit(solution)/shard_map/rgp,gpk->grk/dot_general | solution.py:52
  16.5 0.0 copy-start.1
  16.5 1.7 %fusion.35 = f32[16,16,64]{2,1,0:T(8,128)S(1)} fusion(f32[16,16,64]{2,1,0:T(8,128)S(1)} %fusion.34, f32[16,64,64]{2,1,0:T(8,128)} %param.25), kind=kOutput, calls=%fused_computation.71 | convolution fusion | flops 12582912 | bytes 393216 | tf_op jit(solution)/shard_map/grk,gkl->grl/dot_general | solution.py:53
  18.1 0.2 fusion.12
  18.3 0.1 collective-permute-start
  18.4 6.0 %collective-permute-start.1 = (f32[8,16,64]{2,0,1:T(8,128)S(1)}, f32[8,16,64]{2,0,1:T(8,128)S(1)}, u32[]{:S(2)}, u32[]{:S(2)}) collective-permute-start(f32[8,16,64]{2,0,1:T(8,128)S(1)} %fusion.12), channel_id=1, source_target_pairs={{1,0},{2,1},{3,2},{4,3},{5,4},{6,5},{7,6},{8,7},{9,8},{10,9},{11,1... | collective-permute-start | bytes 98312 | tf_op jit(solution)/shard_map/ppermute | solution.py:18
  24.4 0.3 copy.71
  24.7 0.1 collective-permute-start.2
  24.7 6.0 %collective-permute-start.3 = (bf16[16,4096]{1,0:T(8,128)(2,1)S(1)}, bf16[16,4096]{1,0:T(8,128)(2,1)S(1)}, u32[]{:S(2)}, u32[]{:S(2)}) collective-permute-start(bf16[16,4096]{1,0:T(8,128)(2,1)S(1)} %copy.71), channel_id=1, source_target_pairs={{1,0},{2,1},{3,2},{4,3},{5,4},{6,5},{7,6},{8,7},{9,8},{10,9},{11,1... | collective-permute-start | bytes 393224 | tf_op jit(solution)/shard_map/ppermute | solution.py:18
  30.7 0.7 compare_select_fusion.2
  31.4 0.1 copy.66
  31.5 0.1 reshape.72
  31.6 1.2 %convolution_bitcast_fusion.5 = f32[16,64]{1,0:T(8,128)S(1)} fusion(f32[8,64,64]{2,1,0:T(8,128)} %param.26, f32[8,16,64]{2,0,1:T(8,128)S(1)} %fusion.12), kind=kOutput, calls=%fused_computation.16 | convolution fusion | flops 6291456 | bytes 167936 | tf_op jit(solution)/shard_map/crk,ckl->rl/dot_general | solution.py:57
  32.8 12.8 %all-gather = f32[128,64]{1,0:T(8,128)S(1)} all-gather(f32[16,64]{1,0:T(8,128)S(1)} %convolution_bitcast_fusion.5), channel_id=2, replica_groups=mesh['branch'=16,'leaf'=8] {'leaf'}, dimensions={0}, use_global_device_ids=true | all-gather | bytes 36864 | tf_op jit(solution)/shard_map/all_gather | solution.py:60
  45.5 0.9 fusion.21
  46.4 12.7 %all-gather.1 = f32[128,64]{1,0:T(8,128)S(1)} all-gather(f32[16,64]{1,0:T(8,128)S(1)} %fusion.21), channel_id=3, replica_groups=mesh['branch'=16,'leaf'=8] {'leaf'}, dimensions={0}, use_global_device_ids=true | all-gather | bytes 36864 | tf_op jit(solution)/shard_map/all_gather | solution.py:61
  59.2 24.5 %all-gather.2 = f32[256,64]{1,0:T(8,128)S(1)} all-gather(f32[16,64]{1,0:T(8,128)S(1)} %reduce_sum.9), channel_id=4, replica_groups=mesh['branch'=16,'leaf'=8] {'branch'}, dimensions={0}, use_global_device_ids=true | all-gather | bytes 69632 | tf_op jit(solution)/shard_map/all_gather | solution.py:64
  83.7 0.7 convert_bitcast_fusion
  84.3 0.7 convert_bitcast_fusion.1
  85.0 0.7 compare_select_fusion.1
  85.7 0.1 copy.74
  85.8 0.1 reshape.80
  85.9 0.7 fusion.25
  86.6 1.5 %convolution_bitcast_fusion.3 = f32[16,64]{1,0:T(8,128)S(1)} fusion(f32[1,16,64,64]{3,2,1,0:T(8,128)} %param.30, f32[16,16,64]{2,1,0:T(8,128)S(1)} %bitcast.80, f32[16]{0:T(128)S(1)} %convert_bitcast_fusion), kind=kOutput, calls=%fused_computation.14 | convolution fusion | flops 12599296 | bytes 331840 | tf_op jit(solution)/shard_map/bj,jrk,bjkl->rl/dot_general | solution.py:65
  88.1 1.3 %convolution_bitcast_fusion.4 = f32[16,64]{1,0:T(8,128)S(1)} fusion(f32[1,8,64,64]{3,2,1,0:T(8,128)} %param.29, f32[8,16,64]{2,1,0:T(8,128)S(1)} %bitcast.82, f32[8]{0:T(128)S(1)} %convert_bitcast_fusion.1), kind=kOutput, calls=%fused_computation.15 | convolution fusion | flops 6299648 | bytes 167968 | tf_op jit(solution)/shard_map/dj,jrk,djkl->rl/dot_general | solution.py:68
  89.4 0.9 fusion.3
  90.3 0.0 collective-permute-done
  90.4 0.0 collective-permute-done.1
  90.4 0.6 gather_fusion.1
  91.0 0.0 copy-done
  91.0 0.7 convolution_bitcast_fusion.2
  91.7 1.7 %fusion.2 = f32[8,16,64]{2,1,0:T(8,128)S(1)} fusion(f32[8,16,64]{2,1,0:T(8,128)S(1)} %convolution_bitcast_fusion.2, f32[16,64,1]{1,0,2:T(8,128)S(1)} %fusion.3, f32[8,64,64]{2,1,0:T(8,128)} %param.26), kind=kOutput, calls=%fused_computation.10 | convolution fusion | flops 6299648 | bytes 200704 | tf_op jit(solution)/shard_map/rl,ckl->crk/dot_general | solution.py:75
  93.4 0.3 fusion.15
  93.6 2.0 %convolution_convert_fusion = bf16[16,16,64]{2,1,0:T(8,128)(2,1)S(1)} fusion(f32[16,64,64]{2,1,0:T(8,128)} %param.25, f32[16,16,64]{2,0,1:T(8,128)S(1)} %fusion.15), kind=kOutput, calls=%fused_computation.8 | convolution fusion | flops 12599296 | bytes 360448 | tf_op jit(solution)/shard_map/grl,gkl->grk/dot_general | solution.py:79
  95.6 0.0 collective-permute-done.2
  95.6 0.0 collective-permute-done.3
  95.7 0.6 gather_fusion.2
  96.3 6.4 %convolution_bitcast_fusion = f32[16,16,256]{2,1,0:T(8,128)S(1)} fusion(bf16[16,6,256,256]{3,2,1,0:T(8,128)(2,1)} %param.31, bf16[16,6,16,256]{3,2,1,0:T(8,128)(2,1)S(1)} %bitcast.76, bf16[16,6]{1,0:T(8,128)(2,1)S(1)} %fusion.25), kind=kOutput, calls=%fused_computation.5 | convolution fusion | flops 201719808 | bytes 13631680 | tf_op jit(solution)/shard_map/rgsq,gsqp->rgp/dot_general | solution.py:88
  102.7 0.0 copy-done.1
  102.7 0.2 fusion.1
  102.9 0.5 copy.77
  103.4 11.1 %scatter_custom_fusion = bf16[16,4096]{0,1:T(8,128)(2,1)S(1)} fusion(s32[4096]{0:T(1024)S(1)} %get-tuple-element.6, bf16[4096,16]{1,0:T(8,128)(2,1)S(1)} %copy.77, bf16[]{:T(256)} %constant.66.clone.1), kind=kCustom, calls=%fused_computation.20 | custom fusion | bytes 131074 | tf_op jit(solution)/shard_map/scatter | solution.py:90
  114.5 1.0 copy.78
  (8 shorter events, 0.2 us)
Async XLA Ops:
  0.0 91.0 %copy-start = (f32[8,4,64,64]{3,2,1,0:T(8,128)S(1)}, f32[8,4,64,64]{3,2,1,0:T(8,128)}, u32[]{:S(2)}) copy-start(f32[8,4,64,64]{3,2,1,0:T(8,128)} %param.28) | copy-start | bytes 1572868
  16.5 86.2 %copy-start.1 = (bf16[16,256,64]{1,2,0:T(8,128)(2,1)S(1)}, bf16[16,256,64]{1,2,0:T(8,128)(2,1)}, u32[]{:S(2)}) copy-start(bf16[16,256,64]{1,2,0:T(8,128)(2,1)} %param.24) | copy-start | bytes 1572868
  18.3 72.0 %collective-permute-start = (f32[8,16,64]{2,0,1:T(8,128)S(1)}, f32[8,16,64]{2,0,1:T(8,128)S(1)}, u32[]{:S(2)}, u32[]{:S(2)}) collective-permute-start(f32[8,16,64]{2,0,1:T(8,128)S(1)} %fusion.12), channel_id=1, source_target_pairs={{0,1},{1,2},{2,3},{3,4},{4,5},{5,6},{6,7},{7,8},{8,9},{9,10},{10,1... | collective-permute-start | bytes 98312 | tf_op jit(solution)/shard_map/ppermute | solution.py:15
  18.4 71.9 %collective-permute-start.1 = (f32[8,16,64]{2,0,1:T(8,128)S(1)}, f32[8,16,64]{2,0,1:T(8,128)S(1)}, u32[]{:S(2)}, u32[]{:S(2)}) collective-permute-start(f32[8,16,64]{2,0,1:T(8,128)S(1)} %fusion.12), channel_id=1, source_target_pairs={{1,0},{2,1},{3,2},{4,3},{5,4},{6,5},{7,6},{8,7},{9,8},{10,9},{11,1... | collective-permute-start | bytes 98312 | tf_op jit(solution)/shard_map/ppermute | solution.py:18
  24.7 70.9 %collective-permute-start.2 = (bf16[16,4096]{1,0:T(8,128)(2,1)S(1)}, bf16[16,4096]{1,0:T(8,128)(2,1)S(1)}, u32[]{:S(2)}, u32[]{:S(2)}) collective-permute-start(bf16[16,4096]{1,0:T(8,128)(2,1)S(1)} %copy.71), channel_id=1, source_target_pairs={{0,1},{1,2},{2,3},{3,4},{4,5},{5,6},{6,7},{7,8},{8,9},{9,10},{10,1... | collective-permute-start | bytes 393224 | tf_op jit(solution)/shard_map/ppermute | solution.py:15
  24.7 70.9 %collective-permute-start.3 = (bf16[16,4096]{1,0:T(8,128)(2,1)S(1)}, bf16[16,4096]{1,0:T(8,128)(2,1)S(1)}, u32[]{:S(2)}, u32[]{:S(2)}) collective-permute-start(bf16[16,4096]{1,0:T(8,128)(2,1)S(1)} %copy.71), channel_id=1, source_target_pairs={{1,0},{2,1},{3,2},{4,3},{5,4},{6,5},{7,6},{8,7},{9,8},{10,9},{11,1... | collective-permute-start | bytes 393224 | tf_op jit(solution)/shard_map/ppermute | solution.py:18
where the time goes:
time: 116 us
  blocking collectives  50 us (43%)
  local copies, waits for them, and re-layouts  28 us (24%)
  matrix products  20.2 us (17%)
  starting transfers between devices  12 us (10%)
  other arithmetic  5.03 us (4%)
    all_gather x1, blocking collectives, body(): subtree_coef = lax.all_gather(own_root, 'branch', axis=0, tiled=True)  24.5 us
    all_gather x1, blocking collectives, body(): lax.all_gather(device_coef, 'leaf', axis=0, tiled=True)  12.8 us
    all_gather x1, blocking collectives, body(): lax.all_gather(raised, 'leaf', axis=0, tiled=True)  12.7 us
    gather x2, local copies, waits for them, and re-layouts, body(): sorted_rhs = points_rhs[:, local_order]  12.4 us
    scatter x2, local copies, waits for them, and re-layouts, body(): return jnp.zeros_like(points_rhs).at[:, local_order].set(leaf_out)  12.1 us
    ppermute x2, starting transfers between devices, with_halo(): lax.ppermute(lax.slice_in_dim(block, 0, width, axis=dim), axis, backward)  11.9 us
    dot_general x1, matrix products, body(): jnp.einsum('rgsq,gsqp->rgp', picked, near_tiles, preferred_element_type=j...  6.35 us
  transfers between devices with their start and end apart: 4, of which 0 were waited for; matrix products, arithmetic and copies ran while one was open for 13% of the time, Pallas kernels for 0%

commit v1 on v0

v1 whole, which is shorter than its diff:
```python
import functools

import jax
import jax.numpy as jnp
from jax import lax
from jax.experimental import pallas as pl
from jax.experimental.pallas import tpu as pltpu
from jax.sharding import PartitionSpec as P

MESH = pl.DeviceIdType.MESH
HIGH = lax.Precision.HIGHEST
F32 = jnp.float32
BF16 = jnp.bfloat16
NN = (((1,), (0,)), ((), ()))
NT = (((1,), (1,)), ((), ()))
EARLY = 6


def dot(a, b, dims=NN):
    return lax.dot_general(a, b, dims, preferred_element_type=F32)


def halves(a):
    high = a.astype(BF16)
    return high, (a - high.astype(F32)).astype(BF16)


def split(a):
    return jnp.concatenate(halves(a), axis=1)


def stacked(w):
    high, low = halves(w)
    return jnp.concatenate([high, high, low, low], axis=0)


def times(a, w):
    return dot(jnp.concatenate([a, a], axis=1), w)


def kernel(
    nb,
    nl,
    parent_s,
    near_s,
    count_s,
    far_s,
    mask2_s,
    mask3_s,
    x_h,
    order_h,
    basis_h,
    t1_h,
    t2_h,
    t3_h,
    c1_h,
    c2_h,
    c3_h,
    tiles_h,
    out_h,
    x_v,
    order_v,
    basis_v,
    t1_v,
    t2_v,
    t3_v,
    c1_v,
    c2_v,
    c3_v,
    tiles_v,
    pick_v,
    window,
    clusters,
    field_v,
    near_v,
    group,
    roots,
    out_v,
    in_sem,
    tile_sem,
    x_send,
    x_recv,
    c_send,
    c_recv,
    g_send,
    g_recv,
    r_send,
    r_recv,
    out_sem,
):
    leaves, rank, size = basis_v.shape
    slots = tiles_v.shape[1]
    count = t2_v.shape[0]
    far = c1_v.shape[1]
    rows = x_v.shape[0]
    half = leaves // 2
    total = nb * nl
    b = lax.axis_index("branch")
    j = lax.axis_index("leaf")
    d = b * nl + j
    right = lax.rem(d + 1, total)
    left = lax.rem(d + total - 1, total)
    right_id = (right // nl, lax.rem(right, nl))
    left_id = (left // nl, lax.rem(left, nl))

    loads = [
        pltpu.make_async_copy(src, dst, in_sem.at[i])
        for i, (src, dst) in enumerate(
            [
                (order_h, order_v),
                (x_h, x_v),
                (basis_h, basis_v),
                (t1_h, t1_v),
                (t2_h, t2_v),
                (t3_h, t3_v),
                (c2_h, c2_v),
                (c1_h, c1_v),
                (c3_h, c3_v),
            ]
        )
    ]
    for load in loads:
        load.start()
    tile_loads = [
        pltpu.make_async_copy(tiles_h.at[g], tiles_v.at[g], tile_sem.at[g]) for g in range(leaves)
    ]
    for load in tile_loads:
        load.start()

    barrier = pltpu.get_barrier_semaphore()
    peers = [left_id, right_id]
    peers += [(b, lax.rem(j + i, nl)) for i in range(1, nl)]
    peers += [(lax.rem(b + i, nb), j) for i in range(1, nb)]
    for peer in peers:
        pl.semaphore_signal(barrier, inc=1, device_id=peer, device_id_type=MESH)

    loads[0].wait()
    loads[1].wait()
    order = order_v[...]
    low = jnp.bitwise_and(order, size - 1)
    high = jnp.bitwise_and(jnp.right_shift(order, size.bit_length() - 1), leaves - 1)
    x_all = x_v[...]
    blocks = jnp.concatenate([x_all[:, h * size : (h + 1) * size] for h in range(leaves)], axis=0)
    spot = lax.broadcasted_iota(jnp.int32, (size, size), 0)
    for g in range(leaves):
        cols = slice(g * size, (g + 1) * size)
        onehot = (spot == low[:, cols]).astype(F32).astype(BF16)
        pick_v[g] = onehot
        spread = dot(blocks, onehot)
        chosen = jnp.zeros((rows, size), F32)
        for h in range(leaves):
            chosen = jnp.where(high[:, cols] == h, spread[h * rows : (h + 1) * rows], chosen)
        window[half + g] = chosen.astype(BF16)
    window[2 * leaves] = jnp.zeros((rows, size), BF16)

    pl.semaphore_wait(barrier, len(peers))
    x_copies = [
        pltpu.make_async_remote_copy(
            src_ref=window.at[pl.ds(leaves, half)],
            dst_ref=window.at[pl.ds(0, half)],
            send_sem=x_send.at[0],
            recv_sem=x_recv.at[0],
            device_id=right_id,
            device_id_type=MESH,
        ),
        pltpu.make_async_remote_copy(
            src_ref=window.at[pl.ds(half, half)],
            dst_ref=window.at[pl.ds(half + leaves, half)],
            send_sem=x_send.at[1],
            recv_sem=x_recv.at[1],
            device_id=left_id,
            device_id_type=MESH,
        ),
    ]
    for copy in x_copies:
        copy.start()

    loads[2].wait()
    loads[3].wait()
    parts = [jnp.zeros((rows, rank), F32) for _ in range(count)]
    for g in range(leaves):
        coef = dot(window[half + g], basis_v[g], NT)
        moved = times(split(coef), stacked(t1_v[g]))
        own = jnp.bitwise_and(parent_s[g], count - 1)
        for c in range(count):
            parts[c] = parts[c] + jnp.where(own == c, moved, 0.0)
    parts = [split(part) for part in parts]
    for c in range(count):
        clusters[count + c] = parts[c]
    loads[4].wait()
    loads[5].wait()
    root = times(parts[0], stacked(t2_v[0]))
    for c in range(1, count):
        root = root + times(parts[c], stacked(t2_v[c]))
    root = split(root)
    raised = split(times(root, stacked(t3_v[0])))
    group[j] = jnp.concatenate([root, raised], axis=0)
    g_copies = []
    for i in range(1, nl):
        g_copies.append(
            pltpu.make_async_remote_copy(
                src_ref=group.at[j],
                dst_ref=group.at[j],
                send_sem=g_send.at[i],
                recv_sem=g_recv.at[j],
                device_id=(b, lax.rem(j + i, nl)),
                device_id_type=MESH,
            )
        )
        g_copies[-1].start()
    c_copies = [
        pltpu.make_async_remote_copy(
            src_ref=clusters.at[pl.ds(count, count)],
            dst_ref=clusters.at[pl.ds(0, count)],
            send_sem=c_send.at[0],
            recv_sem=c_recv.at[0],
            device_id=right_id,
            device_id_type=MESH,
        ),
        pltpu.make_async_remote_copy(
            src_ref=clusters.at[pl.ds(count, count)],
            dst_ref=clusters.at[pl.ds(2 * count, count)],
            send_sem=c_send.at[1],
            recv_sem=c_recv.at[1],
            device_id=left_id,
            device_id_type=MESH,
        ),
    ]
    for copy in c_copies:
        copy.start()

    for copy in x_copies:
        copy.wait_recv()

    def near(g):
        pltpu.make_async_copy(tiles_h.at[g], tiles_v.at[g], tile_sem.at[g]).wait()
        picked = []
        for s in range(slots):
            at = jnp.bitwise_and(near_s[s, g] - d * leaves + half, total * leaves - 1)
            at = jnp.where(s < count_s[g], at, 2 * leaves)
            picked.append(window[jnp.minimum(at, 2 * leaves)])
        near_v[g] = dot(
            jnp.concatenate(picked, axis=1), tiles_v[g].reshape(slots * size, size)
        )

    def near_step(g, carry):
        near(g)
        return carry

    lax.fori_loop(0, EARLY, near_step, 0)

    def await_group(i, carry):
        src = lax.rem(j + i, nl)
        pltpu.make_async_remote_copy(
            src_ref=group.at[src],
            dst_ref=group.at[src],
            send_sem=g_send.at[0],
            recv_sem=g_recv.at[src],
            device_id=(b, src),
            device_id_type=MESH,
        ).wait_recv()
        return carry

    for i in range(1, nl):
        await_group(i, 0)
    subtree = group[0, rows:].astype(F32)
    for i in range(1, nl):
        subtree = subtree + group[i, rows:].astype(F32)
    subtree = subtree[:, :rank] + subtree[:, rank:]
    roots[b] = split(subtree)
    r_copies = []
    for i in range(1, nb):
        r_copies.append(
            pltpu.make_async_remote_copy(
                src_ref=roots.at[b],
                dst_ref=roots.at[b],
                send_sem=r_send.at[i],
                recv_sem=r_recv.at[b],
                device_id=(lax.rem(b + i, nb), j),
                device_id_type=MESH,
            )
        )
        r_copies[-1].start()

    lax.fori_loop(EARLY, leaves, near_step, 0)

    loads[6].wait()
    field = jnp.zeros((rows, rank), F32)
    for i in range(nl):
        field = field + mask2_s[0, i].astype(F32) * times(group[i, :rows], stacked(c2_v[0, i]))
    loads[7].wait()
    for copy in c_copies:
        copy.wait_recv()
    cross = []
    for c in range(count):
        part = jnp.zeros((rows, rank), F32)
        for s in range(far):
            at = jnp.bitwise_and(far_s[s, c] - (d - 1) * count, total * count - 1)
            part = part + times(clusters[jnp.minimum(at, 3 * count - 1)], stacked(c1_v[c, s]))
        cross.append(part)

    loads[8].wait()
    for i in range(1, nb):
        src = lax.rem(b + i, nb)
        pltpu.make_async_remote_copy(
            src_ref=roots.at[src],
            dst_ref=roots.at[src],
            send_sem=r_send.at[0],
            recv_sem=r_recv.at[src],
            device_id=(src, j),
            device_id_type=MESH,
        ).wait_recv()
    top = jnp.zeros((rows, rank), F32)
    for i in range(nb):
        top = top + mask3_s[0, i].astype(F32) * times(roots[i], stacked(c3_v[0, i]))

    field = split(field + times(split(top), stacked(t3_v[0].T)))
    for c in range(count):
        field_v[c] = split(cross[c] + times(field, stacked(t2_v[c].T)))
    product = jnp.zeros((leaves * rows, size), F32)
    for g in range(leaves):
        cols = slice(g * size, (g + 1) * size)
        own = jnp.bitwise_and(parent_s[g], count - 1)
        leaf = times(field_v[own], stacked(t1_v[g].T)).astype(BF16)
        leaf_out = (dot(leaf, basis_v[g]) + near_v[g]).astype(BF16).astype(F32)
        spread = jnp.concatenate(
            [jnp.where(high[:, cols] == h, leaf_out, 0.0).astype(BF16) for h in range(leaves)],
            axis=0,
        )
        product = product + dot(spread, pick_v[g], NT)
    for h in range(leaves):
        out_v[:, h * size : (h + 1) * size] = product[h * rows : (h + 1) * rows].astype(BF16)
    store = pltpu.make_async_copy(out_v, out_h, out_sem)
    store.start()
    for copy in x_copies + g_copies + c_copies + r_copies:
        copy.wait_send()
    store.wait()


def body(
    points_rhs,
    order,
    leaf_parent,
    near_list,
    near_count,
    far_list,
    pair_mask2,
    pair_mask3,
    basis,
    transfer1,
    transfer2,
    transfer3,
    couple1,
    couple2,
    couple3,
    near_tiles,
):
    rows, points = points_rhs.shape
    leaves, size, rank = basis.shape
    count = transfer2.shape[0]
    nb, nl = lax.axis_size("branch"), lax.axis_size("leaf")
    smem = pl.BlockSpec(memory_space=pltpu.SMEM)
    hbm = pl.BlockSpec(memory_space=pl.ANY)
    dma = pltpu.SemaphoreType.DMA
    operands = (
        points_rhs,
        order.reshape(1, points),
        jnp.swapaxes(basis, 1, 2),
        transfer1,
        transfer2,
        transfer3,
        couple1,
        couple2,
        couple3,
        near_tiles,
    )
    return pl.pallas_call(
        functools.partial(kernel, nb, nl),
        out_shape=jax.ShapeDtypeStruct(points_rhs.shape, points_rhs.dtype),
        in_specs=[smem] * 6 + [hbm] * len(operands),
        out_specs=hbm,
        scratch_shapes=[pltpu.VMEM(a.shape, a.dtype) for a in operands]
        + [
            pltpu.VMEM((leaves, size, size), BF16),
            pltpu.VMEM((2 * leaves + 1, rows, size), BF16),
            pltpu.VMEM((3 * count, rows, 2 * rank), BF16),
            pltpu.VMEM((count, rows, 2 * rank), BF16),
            pltpu.VMEM((leaves, rows, size), F32),
            pltpu.VMEM((nl, 2 * rows, 2 * rank), BF16),
            pltpu.VMEM((nb, rows, 2 * rank), BF16),
            pltpu.VMEM(points_rhs.shape, points_rhs.dtype),
            dma((len(operands) - 1,)),
            dma((leaves,)),
            dma((2,)),
            dma((2,)),
            dma((2,)),
            dma((2,)),
            dma((nl,)),
            dma((nl,)),
            dma((nb,)),
            dma((nb,)),
            dma(()),
        ],
        compiler_params=pltpu.CompilerParams(
            collective_id=0, has_side_effects=True, vmem_limit_bytes=40 * 2**20
        ),
    )(
        leaf_parent,
        near_list.T,
        near_count,
        far_list.T,
        pair_mask2,
        pair_mask3,
        *operands,
    )


def solution(mesh):
    both = ("branch", "leaf")
    return jax.shard_map(
        body,
        mesh=mesh,
        in_specs=(
            P(None, both),
            P(both),
            P(both),
            P(both, None),
            P(both),
            P(both, None),
            P(both, None),
            P("branch", None),
            P(both, None, None),
            P(both, None, None),
            P(both, None, None),
            P(both, None, None),
            P(both, None, None, None),
            P(both, None, None, None),
            P("branch", None, None, None),
            P(both, None, None, None),
        ),
        out_specs=P(None, both),
        check_vma=False,
    )
```

time: 116 us -> 37.6 us (0.32)
  the two profiles are of different devices: /device:TPU:8 before, /device:TPU:7 now
where the time goes in v1:
time: 37.6 us; the launch traced here: 37 us
  Pallas kernels  23.7 us (63%)
  local copies, waits for them, and re-layouts  13.3 us (35%)
    pallas_call x1, Pallas kernels, body(): pl.pallas_call(functools.partial(kernel, nb, nl), out_shape=jax.ShapeDtyp...  23.7 us
    unnamed x31, local copies, waits for them, and re-layouts  13.3 us

profile of v1, /device:TPU:7, one launch (start us, length us, event | category | flops | bytes accessed | tf_op | source)
XLA Modules:
  0.0 37.0 jit_solution(1970402512436791990)
XLA Ops:
  0.0 0.0 copy-start
  0.0 1.2 %copy-done = f32[8,4,64,64]{3,2,1,0:T(8,128)S(1)} copy-done((f32[8,4,64,64]{3,2,1,0:T(8,128)S(1)}, f32[8,4,64,64]{3,2,1,0:T(8,128)}, u32[]{:S(2)}) %copy-start) | copy-done | bytes 524312
  1.2 0.0 copy-start.1
  1.2 1.0 %copy-done.1 = bf16[16,256,64]{1,2,0:T(8,128)(2,1)S(1)} copy-done((bf16[16,256,64]{1,2,0:T(8,128)(2,1)S(1)}, bf16[16,256,64]{1,2,0:T(8,128)(2,1)}, u32[]{:S(2)}) %copy-start.1) | copy-done | bytes 524312
  2.3 0.0 copy-start.2
  2.3 1.0 %copy-done.2 = f32[16,64,64]{2,1,0:T(8,128)S(1)} copy-done((f32[16,64,64]{2,1,0:T(8,128)S(1)}, f32[16,64,64]{2,1,0:T(8,128)}, u32[]{:S(2)}) %copy-start.2) | copy-done | bytes 262168
  3.3 0.0 copy-start.3
  3.3 1.0 %copy-done.3 = f32[1,16,64,64]{3,2,1,0:T(8,128)S(1)} copy-done((f32[1,16,64,64]{3,2,1,0:T(8,128)S(1)}, f32[1,16,64,64]{3,2,1,0:T(8,128)}, u32[]{:S(2)}) %copy-start.3) | copy-done | bytes 262168
  4.4 0.0 copy-start.4
  4.4 0.9 %copy-done.4 = f32[8,64,64]{2,1,0:T(8,128)S(1)} copy-done((f32[8,64,64]{2,1,0:T(8,128)S(1)}, f32[8,64,64]{2,1,0:T(8,128)}, u32[]{:S(2)}) %copy-start.4) | copy-done | bytes 131096
  5.3 0.0 copy-start.5
  5.3 0.9 %copy-done.5 = f32[1,8,64,64]{3,2,1,0:T(8,128)S(1)} copy-done((f32[1,8,64,64]{3,2,1,0:T(8,128)S(1)}, f32[1,8,64,64]{3,2,1,0:T(8,128)}, u32[]{:S(2)}) %copy-start.5) | copy-done | bytes 131096
  6.3 0.0 copy-start.6
  6.3 0.9 %copy-done.6 = bf16[16,4096]{1,0:T(8,128)(2,1)S(1)} copy-done((bf16[16,4096]{1,0:T(8,128)(2,1)S(1)}, bf16[16,4096]{1,0:T(8,128)(2,1)}, u32[]{:S(2)}) %copy-start.6) | copy-done | bytes 131096
  7.2 0.0 copy-start.7
  7.2 0.8 %copy-done.7 = f32[1,64,64]{2,1,0:T(8,128)S(1)} copy-done((f32[1,64,64]{2,1,0:T(8,128)S(1)}, f32[1,64,64]{2,1,0:T(8,128)}, u32[]{:S(2)}) %copy-start.7) | copy-done | bytes 16408
  7.9 0.0 copy-start.8
  7.9 0.7 %copy-done.8 = s32[4096]{0:T(1024)S(1)} copy-done((s32[4096]{0:T(1024)S(1)}, s32[4096]{0:T(1024)}, u32[]{:S(2)}) %copy-start.8) | copy-done | bytes 16408
  8.6 0.0 copy-start.9
  8.6 0.7 %copy-done.9 = s32[16,6]{0,1:T(8,128)S(1)} copy-done((s32[16,6]{0,1:T(8,128)S(1)}, s32[16,6]{0,1:T(8,128)}, u32[]{:S(2)}) %copy-start.9) | copy-done | bytes 408
  9.3 0.0 copy-start.10
  9.3 0.7 %copy-done.10 = s32[8,4]{0,1:T(4,128)S(1)} copy-done((s32[8,4]{0,1:T(4,128)S(1)}, s32[8,4]{0,1:T(4,128)}, u32[]{:S(2)}) %copy-start.10) | copy-done | bytes 152
  10.0 0.0 copy-start.11
  10.0 0.7 %copy-done.11 = s32[16]{0:T(128)S(1)} copy-done((s32[16]{0:T(128)S(1)}, s32[16]{0:T(128)}, u32[]{:S(2)}) %copy-start.11) | copy-done | bytes 88
  10.7 0.0 copy-start.12
  10.7 0.7 %copy-done.12 = s32[16]{0:T(128)S(1)} copy-done((s32[16]{0:T(128)S(1)}, s32[16]{0:T(128)}, u32[]{:S(2)}) %copy-start.12) | copy-done | bytes 88
  11.3 0.0 copy-start.13
  11.3 0.7 %copy-done.13 = s32[1,8]{1,0:T(1,128)S(1)} copy-done((s32[1,8]{1,0:T(1,128)S(1)}, s32[1,8]{1,0:T(1,128)}, u32[]{:S(2)}) %copy-start.13) | copy-done | bytes 56
  12.0 0.0 copy-start.14
  12.0 0.7 %copy-done.14 = s32[1,16]{1,0:T(1,128)S(1)} copy-done((s32[1,16]{1,0:T(1,128)S(1)}, s32[1,16]{1,0:T(1,128)}, u32[]{:S(2)}) %copy-start.14) | copy-done | bytes 88
  12.6 23.7 %shard_map.154 = bf16[16,4096]{1,0:T(8,128)(2,1)S(1)} custom-call(s32[16]{0:T(128)S(1)} %copy-done.11, s32[6,16]{1,0:T(8,128)S(1)} %bitcast.6, s32[16]{0:T(128)S(1)} %copy-done.12, s32[4,8]{1,0:T(4,128)S(1)} %bitcast.7, s32[1,8]{1,0:T(1,128)S(1)} %copy-done.13, s32[1,16]{1,0:T(1,128)S(1)} %copy-done.14, bf16[16,4096]{1,0:T(8,128)(2,1)S(1)} %copy-done.6, ...), custom_call_target="tpu_custom_call" | custom-call | tf_op jit(solution)/shard_map/pallas_call | solution.py:377
  36.4 0.7 %copy.18 = bf16[16,4096]{1,0:T(8,128)(2,1)} copy(bf16[16,4096]{1,0:T(8,128)(2,1)S(1)} %shard_map.154) | data formatting | bytes 262144
Async XLA Ops:
  0.0 1.2 %copy-start = (f32[8,4,64,64]{3,2,1,0:T(8,128)S(1)}, f32[8,4,64,64]{3,2,1,0:T(8,128)}, u32[]{:S(2)}) copy-start(f32[8,4,64,64]{3,2,1,0:T(8,128)} %c1_h.1) | copy-start | bytes 1572868
  1.2 1.0 %copy-start.1 = (bf16[16,256,64]{1,2,0:T(8,128)(2,1)S(1)}, bf16[16,256,64]{1,2,0:T(8,128)(2,1)}, u32[]{:S(2)}) copy-start(bf16[16,256,64]{1,2,0:T(8,128)(2,1)} %param.24) | copy-start | bytes 1572868
  2.3 1.0 %copy-start.2 = (f32[16,64,64]{2,1,0:T(8,128)S(1)}, f32[16,64,64]{2,1,0:T(8,128)}, u32[]{:S(2)}) copy-start(f32[16,64,64]{2,1,0:T(8,128)} %t1_h.1) | copy-start | bytes 786436
  3.3 1.0 %copy-start.3 = (f32[1,16,64,64]{3,2,1,0:T(8,128)S(1)}, f32[1,16,64,64]{3,2,1,0:T(8,128)}, u32[]{:S(2)}) copy-start(f32[1,16,64,64]{3,2,1,0:T(8,128)} %c3_h.1) | copy-start | bytes 786436
  4.4 0.9 %copy-start.4 = (f32[8,64,64]{2,1,0:T(8,128)S(1)}, f32[8,64,64]{2,1,0:T(8,128)}, u32[]{:S(2)}) copy-start(f32[8,64,64]{2,1,0:T(8,128)} %t2_h.1) | copy-start | bytes 393220
  5.3 0.9 %copy-start.5 = (f32[1,8,64,64]{3,2,1,0:T(8,128)S(1)}, f32[1,8,64,64]{3,2,1,0:T(8,128)}, u32[]{:S(2)}) copy-start(f32[1,8,64,64]{3,2,1,0:T(8,128)} %c2_h.1) | copy-start | bytes 393220
  6.3 0.9 %copy-start.6 = (bf16[16,4096]{1,0:T(8,128)(2,1)S(1)}, bf16[16,4096]{1,0:T(8,128)(2,1)}, u32[]{:S(2)}) copy-start(bf16[16,4096]{1,0:T(8,128)(2,1)} %x_h.1) | copy-start | bytes 393220
  7.2 0.8 %copy-start.7 = (f32[1,64,64]{2,1,0:T(8,128)S(1)}, f32[1,64,64]{2,1,0:T(8,128)}, u32[]{:S(2)}) copy-start(f32[1,64,64]{2,1,0:T(8,128)} %t3_h.1) | copy-start | bytes 49156
  7.9 0.7 %copy-start.8 = (s32[4096]{0:T(1024)S(1)}, s32[4096]{0:T(1024)}, u32[]{:S(2)}) copy-start(s32[4096]{0:T(1024)} %param.17) | copy-start | bytes 49156
  8.6 0.7 %copy-start.9 = (s32[16,6]{0,1:T(8,128)S(1)}, s32[16,6]{0,1:T(8,128)}, u32[]{:S(2)}) copy-start(s32[16,6]{0,1:T(8,128)} %param.19) | copy-start | bytes 1156
  9.3 0.7 %copy-start.10 = (s32[8,4]{0,1:T(4,128)S(1)}, s32[8,4]{0,1:T(4,128)}, u32[]{:S(2)}) copy-start(s32[8,4]{0,1:T(4,128)} %param.21) | copy-start | bytes 388
  10.0 0.7 %copy-start.11 = (s32[16]{0:T(128)S(1)}, s32[16]{0:T(128)}, u32[]{:S(2)}) copy-start(s32[16]{0:T(128)} %parent_s.1) | copy-start | bytes 196
  10.7 0.7 %copy-start.12 = (s32[16]{0:T(128)S(1)}, s32[16]{0:T(128)}, u32[]{:S(2)}) copy-start(s32[16]{0:T(128)} %count_s.1) | copy-start | bytes 196
  11.3 0.7 %copy-start.13 = (s32[1,8]{1,0:T(1,128)S(1)}, s32[1,8]{1,0:T(1,128)}, u32[]{:S(2)}) copy-start(s32[1,8]{1,0:T(1,128)} %mask2_s.1) | copy-start | bytes 100
  12.0 0.7 %copy-start.14 = (s32[1,16]{1,0:T(1,128)S(1)}, s32[1,16]{1,0:T(1,128)}, u32[]{:S(2)}) copy-start(s32[1,16]{1,0:T(1,128)} %mask3_s.1) | copy-start | bytes 196

commit v2 on v1

--- a/solution.py
+++ b/solution.py
@@ -402,7 +402,7 @@
             dma(()),
         ],
         compiler_params=pltpu.CompilerParams(
-            collective_id=0, has_side_effects=True, vmem_limit_bytes=40 * 2**20
+            collective_id=0, has_side_effects=True, vmem_limit_bytes=60 * 2**20
         ),
     )(
         leaf_parent,

time: 37.6 us -> 26.7 us (0.71)
  the two profiles are of different devices: /device:TPU:7 before, /device:TPU:1 now
where the time goes in v2:
time: 26.7 us; the launch traced here: 26.5 us
  Pallas kernels  24.9 us (93%)
  local copies, waits for them, and re-layouts  1.57 us (6%)
    pallas_call x1, Pallas kernels, body(): pl.pallas_call(functools.partial(kernel, nb, nl), out_shape=jax.ShapeDtyp...  24.9 us
    unnamed x1, local copies, waits for them, and re-layouts  1.57 us

profile of v2, /device:TPU:1, one launch (start us, length us, event | category | flops | bytes accessed | tf_op | source)
XLA Modules:
  0.0 26.5 jit_solution(10957640252524898954)
XLA Ops:
  0.0 24.9 %shard_map.154 = bf16[16,4096]{1,0:T(8,128)(2,1)} custom-call(s32[16]{0:T(128)} %parent_s.1, s32[6,16]{1,0:T(8,128)} %bitcast.6, s32[16]{0:T(128)} %count_s.1, s32[4,8]{1,0:T(4,128)} %bitcast.7, s32[1,8]{1,0:T(1,128)} %mask2_s.1, s32[1,16]{1,0:T(1,128)} %mask3_s.1, bf16[16,4096]{1,0:T(8,128)(2,1)} %x_h.1, s32[1,4096]{1,0:T(1,128)} %bitcast.5, ...), custom_call_target="tpu_custom_call" | custom-call | tf_op jit(solution)/shard_map/pallas_call | solution.py:377
  25.0 1.6 %copy.18 = bf16[16,4096]{1,0:T(8,128)(2,1)} copy(bf16[16,4096]{1,0:T(8,128)(2,1)} %shard_map.154) | data formatting | bytes 262144

commit v3 on v2

v3 whole, which is shorter than its diff:
```python
import functools

import jax
import jax.numpy as jnp
from jax import lax
from jax.experimental import pallas as pl
from jax.experimental.pallas import tpu as pltpu
from jax.sharding import PartitionSpec as P

MESH = pl.DeviceIdType.MESH
F32 = jnp.float32
BF16 = jnp.bfloat16
NN = (((1,), (0,)), ((), ()))
NT = (((1,), (1,)), ((), ()))


def dot(a, b, dims=NN):
    return lax.dot_general(a, b, dims, preferred_element_type=F32)


def halves(a):
    high = a.astype(BF16)
    return high, (a - high.astype(F32)).astype(BF16)


def split(a):
    return jnp.concatenate(halves(a), axis=1)


def stacked(w):
    high, low = halves(w)
    return jnp.concatenate([high, high, low, low], axis=0)


def times(a, w):
    return dot(jnp.concatenate([a, a], axis=1), w)


def kernel(
    nb,
    nl,
    x_h,
    order_h,
    basis_h,
    t1_h,
    t2_h,
    t3_h,
    parent_h,
    c1_h,
    c2_h,
    c3_h,
    near_h,
    count_h,
    far_h,
    mask2_h,
    mask3_h,
    tiles_h,
    out_h,
    x_v,
    order_v,
    basis_v,
    t1_v,
    t2_v,
    t3_v,
    parent_s,
    c1_v,
    c2_v,
    c3_v,
    near_s,
    count_s,
    far_s,
    mask2_s,
    mask3_s,
    tiles_v,
    pick_v,
    place_v,
    window,
    clusters,
    lift_v,
    raise_v,
    field_v,
    drop_v,
    c3p_v,
    pre_v,
    near_v,
    raises,
    group,
    roots,
    in_sem,
    tile_sem,
    x_send,
    x_recv,
    c_send,
    c_recv,
    s_send,
    s_recv,
    g_send,
    g_recv,
    r_send,
    r_recv,
):
    leaves, rank, size = basis_v.shape
    slots = tiles_v.shape[1]
    count = t2_v.shape[0]
    far = c1_v.shape[1]
    rows = x_v.shape[0]
    half = leaves // 2
    total = nb * nl
    b = lax.axis_index("branch")
    j = lax.axis_index("leaf")
    d = b * nl + j
    right = lax.rem(d + 1, total)
    left = lax.rem(d + total - 1, total)
    right_id = (right // nl, lax.rem(right, nl))
    left_id = (left // nl, lax.rem(left, nl))

    pairs = [
        (order_h, order_v),
        (x_h, x_v),
        (t3_h, t3_v),
        (t2_h, t2_v),
        (t1_h, t1_v),
        (basis_h, basis_v),
        (parent_h, parent_s),
        (c2_h, c2_v),
        (c1_h, c1_v),
        (c3_h, c3_v),
        (near_h, near_s),
        (count_h, count_s),
        (far_h, far_s),
        (mask2_h, mask2_s),
        (mask3_h, mask3_s),
    ]
    loads = [pltpu.make_async_copy(src, dst, in_sem.at[i]) for i, (src, dst) in enumerate(pairs)]
    for load in loads[:7]:
        load.start()

    barrier = pltpu.get_barrier_semaphore()
    peers = [left_id, right_id]
    peers += [(b, lax.rem(j + i, nl)) for i in range(1, nl)]
    peers += [(lax.rem(b + i, nb), j) for i in range(1, nb)]
    for peer in peers:
        pl.semaphore_signal(barrier, inc=1, device_id=peer, device_id_type=MESH)

    for load in loads[:7]:
        load.wait()
    for load in loads[7:]:
        load.start()
    tile_loads = [
        pltpu.make_async_copy(tiles_h.at[g], tiles_v.at[g], tile_sem.at[g]) for g in range(leaves)
    ]
    for load in tile_loads:
        load.start()

    own = [jnp.bitwise_and(parent_s[g], count - 1) for g in range(leaves)]
    t3_parts = halves(t3_v[0])
    t2_parts = halves(t2_v[...].reshape(count * rank, rank))
    lift = (
        dot(t2_parts[0], t3_parts[0]) + dot(t2_parts[1], t3_parts[0]) + dot(t2_parts[0], t3_parts[1])
    )
    for c in range(count):
        lift_v[c] = stacked(lift[c * rank : (c + 1) * rank])

    order = order_v[...]
    low = jnp.bitwise_and(order, size - 1)
    high = jnp.bitwise_and(jnp.right_shift(order, size.bit_length() - 1), leaves - 1)
    low_short = low.astype(jnp.int16)
    high_short = high.astype(jnp.int16)
    x_all = x_v[...]
    blocks = jnp.concatenate([x_all[:, h * size : (h + 1) * size] for h in range(leaves)], axis=0)
    spot = lax.broadcasted_iota(jnp.int16, (size, size), 0)
    one, zero = jnp.bfloat16(1), jnp.bfloat16(0)
    coefs = []
    raised = jnp.zeros((rows, rank), F32)
    for g in range(leaves):
        cols = slice(g * size, (g + 1) * size)
        onehot = jnp.where(spot == low_short[:, cols], one, zero)
        pick_v[g] = onehot
        spread = dot(blocks, onehot)
        chosen = jnp.zeros((rows, size), F32)
        for h in range(leaves):
            chosen = jnp.where(high[:, cols] == h, spread[h * rows : (h + 1) * rows], chosen)
        chosen = chosen.astype(BF16)
        window[half + g] = chosen
        coefs.append(split(dot(chosen, basis_v[g], NT)))
        direct = times(split(t1_v[g]), lift_v[own[g]])
        raise_v[g] = direct
        raised = raised + times(coefs[g], stacked(direct))
    window[2 * leaves] = jnp.zeros((rows, size), BF16)
    raises[j] = jnp.concatenate([raised, jnp.zeros_like(raised)], axis=1)

    pl.semaphore_wait(barrier, len(peers))
    copies = []

    def send(buffer, at, to, count_, send_sem, recv_sem, device):
        copy = pltpu.make_async_remote_copy(
            src_ref=buffer.at[pl.ds(at, count_)],
            dst_ref=buffer.at[pl.ds(to, count_)],
            send_sem=send_sem,
            recv_sem=recv_sem,
            device_id=device,
            device_id_type=MESH,
        )
        copy.start()
        copies.append(copy)

    def arrive(buffer, at, count_, recv_sem):
        pltpu.make_async_remote_copy(
            src_ref=buffer.at[pl.ds(at, count_)],
            dst_ref=buffer.at[pl.ds(at, count_)],
            send_sem=s_send.at[0],
            recv_sem=recv_sem,
            device_id=right_id,
            device_id_type=MESH,
        ).wait_recv()

    for i in range(1, nl):
        send(raises, j, j, 1, s_send.at[i], s_recv.at[j], (b, lax.rem(j + i, nl)))
    send(window, leaves, 0, half, x_send.at[0], x_recv.at[0], right_id)
    send(window, half, half + leaves, half, x_send.at[1], x_recv.at[1], left_id)

    parts = [jnp.zeros((rows, rank), F32) for _ in range(count)]
    for g in range(leaves):
        moved = times(coefs[g], stacked(t1_v[g]))
        for c in range(count):
            parts[c] = parts[c] + jnp.where(own[g] == c, moved, 0.0)
    parts = [split(part) for part in parts]
    for c in range(count):
        clusters[count + c] = parts[c]
    send(clusters, count, 0, count, c_send.at[0], c_recv.at[0], right_id)
    send(clusters, count, 2 * count, count, c_send.at[1], c_recv.at[1], left_id)
    root = times(parts[0], stacked(t2_v[0]))
    for c in range(1, count):
        root = root + times(parts[c], stacked(t2_v[c]))
    group[j] = split(root)
    for i in range(1, nl):
        send(group, j, j, 1, g_send.at[i], g_recv.at[j], (b, lax.rem(j + i, nl)))

    for i in range(1, nl):
        src = lax.rem(j + i, nl)
        arrive(raises, src, 1, s_recv.at[src])
    subtree = raises[0]
    for i in range(1, nl):
        subtree = subtree + raises[i]
    roots[b] = split(subtree[:, :rank])
    for i in range(1, nb):
        send(roots, b, b, 1, r_send.at[i], r_recv.at[b], (lax.rem(b + i, nb), j))

    for load in loads[7:]:
        load.wait()
    spot_high = jnp.right_shift(spot, rows.bit_length() - 1)
    for g in range(leaves):
        cols = slice(g * size, (g + 1) * size)
        place_v[g] = jnp.where(spot_high == high_short[:, cols], one, zero)
    for i in range(nb):
        weight = c3_v[0, i] * mask3_s[0, i].astype(F32)
        c3p_v[pl.ds(i * 4 * rank, 4 * rank)] = stacked(weight)
    for g in range(leaves // 2):
        drop_v[:, 2 * g * rank : 2 * (g + 1) * rank] = jnp.concatenate(
            [stacked(raise_v[2 * g].T), stacked(raise_v[2 * g + 1].T)], axis=1
        )
    for i in range(1, nl):
        src = lax.rem(j + i, nl)
        arrive(group, src, 1, g_recv.at[src])
    arrive(clusters, 0, count, c_recv.at[0])
    arrive(clusters, 2 * count, count, c_recv.at[1])
    field = jnp.zeros((rows, rank), F32)
    for i in range(nl):
        field = field + mask2_s[0, i].astype(F32) * times(group[i], stacked(c2_v[0, i]))
    field = split(field)
    for c in range(count):
        part = times(field, stacked(t2_v[c].T))
        for s in range(far):
            at = jnp.bitwise_and(far_s[s, c] - (d - 1) * count, total * count - 1)
            part = part + times(clusters[jnp.minimum(at, 3 * count - 1)], stacked(c1_v[c, s]))
        field_v[c] = split(part)
    for g in range(leaves // 2):
        pre_v[:, 2 * g * rank : 2 * (g + 1) * rank] = jnp.concatenate(
            [
                times(field_v[own[2 * g + k]], stacked(t1_v[2 * g + k].T))
                for k in range(2)
            ],
            axis=1,
        )

    arrive(window, 0, half, x_recv.at[0])
    arrive(window, half + leaves, half, x_recv.at[1])
    for load in tile_loads:
        load.wait()
    for g in range(leaves):
        picked = []
        for s in range(slots):
            at = jnp.bitwise_and(near_s[s, g] - d * leaves + half, total * leaves - 1)
            at = jnp.where(s < count_s[g], at, 2 * leaves)
            picked.append(window[jnp.minimum(at, 2 * leaves)])
        near_v[g] = dot(jnp.concatenate(picked, axis=1), tiles_v[g].reshape(slots * size, size))

    for i in range(1, nb):
        src = lax.rem(b + i, nb)
        arrive(roots, src, 1, r_recv.at[src])
    wide = []
    for i in range(nb):
        wide += [roots[i], roots[i]]
    top = split(dot(jnp.concatenate(wide, axis=1), c3p_v[...]))
    leaf = (pre_v[...] + times(top, drop_v[...])).astype(BF16)
    lane = lax.broadcasted_iota(jnp.int32, (rows, 2 * rank), 1)
    product = jnp.zeros((leaves * rows, size), F32)
    for g in range(leaves // 2):
        pair = leaf[:, 2 * g * rank : 2 * (g + 1) * rank].astype(F32)
        both = jnp.concatenate(
            [jnp.where(lane < rank, pair, 0.0), jnp.where(lane < rank, 0.0, pair)], axis=0
        ).astype(BF16)
        points = dot(both, basis_v[pl.ds(2 * g, 2)].reshape(2 * rank, size))
        for k in range(2):
            leaf_out = (points[k * rows : (k + 1) * rows] + near_v[2 * g + k]).astype(BF16)
            spread = jnp.concatenate([leaf_out] * leaves, axis=0) * place_v[2 * g + k]
            product = product + dot(spread, pick_v[2 * g + k], NT)
    for h in range(leaves):
        out_h[:, h * size : (h + 1) * size] = product[h * rows : (h + 1) * rows].astype(BF16)
    for copy in copies:
        copy.wait_send()


def body(
    points_rhs,
    order,
    leaf_parent,
    near_list,
    near_count,
    far_list,
    pair_mask2,
    pair_mask3,
    basis,
    transfer1,
    transfer2,
    transfer3,
    couple1,
    couple2,
    couple3,
    near_tiles,
):
    rows, points = points_rhs.shape
    leaves, size, rank = basis.shape
    count = transfer2.shape[0]
    nb, nl = lax.axis_size("branch"), lax.axis_size("leaf")
    hbm = pl.BlockSpec(memory_space=pl.ANY)
    dma = pltpu.SemaphoreType.DMA
    operands = (
        points_rhs,
        order.reshape(1, points),
        jnp.swapaxes(basis, 1, 2),
        transfer1,
        transfer2,
        transfer3,
        leaf_parent,
        couple1,
        couple2,
        couple3,
        near_list.T,
        near_count,
        far_list.T,
        pair_mask2,
        pair_mask3,
        near_tiles,
    )
    held = [
        (pltpu.SMEM if a.dtype == jnp.int32 and a.size < points else pltpu.VMEM)(a.shape, a.dtype)
        for a in operands
    ]
    return pl.pallas_call(
        functools.partial(kernel, nb, nl),
        out_shape=pltpu.VMEM(points_rhs.shape, points_rhs.dtype),
        in_specs=[hbm] * len(operands),
        out_specs=pl.BlockSpec(memory_space=pltpu.VMEM),
        scratch_shapes=held
        + [
            pltpu.VMEM((leaves, size, size), BF16),
            pltpu.VMEM((leaves, size, size), BF16),
            pltpu.VMEM((2 * leaves + 1, rows, size), BF16),
            pltpu.VMEM((3 * count, rows, 2 * rank), BF16),
            pltpu.VMEM((count, 4 * rank, rank), BF16),
            pltpu.VMEM((leaves, rank, rank), F32),
            pltpu.VMEM((count, rows, 2 * rank), BF16),
            pltpu.VMEM((4 * rank, leaves * rank), BF16),
            pltpu.VMEM((nb * 4 * rank, rank), BF16),
            pltpu.VMEM((rows, leaves * rank), F32),
            pltpu.VMEM((leaves, rows, size), F32),
            pltpu.VMEM((nl, rows, 2 * rank), F32),
            pltpu.VMEM((nl, rows, 2 * rank), BF16),
            pltpu.VMEM((nb, rows, 2 * rank), BF16),
            dma((len(operands) - 1,)),
            dma((leaves,)),
            dma((2,)),
            dma((2,)),
            dma((2,)),
            dma((2,)),
            dma((nl,)),
            dma((nl,)),
            dma((nl,)),
            dma((nl,)),
            dma((nb,)),
            dma((nb,)),
        ],
        compiler_params=pltpu.CompilerParams(
            collective_id=0, has_side_effects=True, vmem_limit_bytes=56 * 2**20
        ),
    )(*[pltpu.with_memory_space_constraint(a, pltpu.HBM) for a in operands])


def solution(mesh):
    both = ("branch", "leaf")
    return jax.shard_map(
        body,
        mesh=mesh,
        in_specs=(
            P(None, both),
            P(both),
            P(both),
            P(both, None),
            P(both),
            P(both, None),
            P(both, None),
            P("branch", None),
            P(both, None, None),
            P(both, None, None),
            P(both, None, None),
            P(both, None, None),
            P(both, None, None, None),
            P(both, None, None, None),
            P("branch", None, None, None),
            P(both, None, None, None),
        ),
        out_specs=P(None, both),
        check_vma=False,
    )
```

time: 26.7 us -> 23.5 us (0.88)
  Pallas kernels: 24.9 us -> 22.7 us
  local copies, waits for them, and re-layouts: 1.57 us -> 0.66 us
    pallas_call x1, Pallas kernels: 24.9 us -> 22.7 us  [body(): pl.pallas_call(functools.partial(kernel, nb, nl), out_shape=pltpu.VMEM(po...]
    unnamed x1, local copies, waits for them, and re-layouts: 1.57 us -> 0.66 us
where the time goes in v3:
time: 23.5 us; the launch traced here: 23.4 us
  Pallas kernels  22.7 us (97%)
  local copies, waits for them, and re-layouts  0.66 us (3%)
    pallas_call x1, Pallas kernels, body(): pl.pallas_call(functools.partial(kernel, nb, nl), out_shape=pltpu.VMEM(po...  22.7 us
    unnamed x1, local copies, waits for them, and re-layouts  0.66 us

profile of v3, /device:TPU:1, one launch (start us, length us, event | category | flops | bytes accessed | tf_op | source)
XLA Modules:
  0.0 23.4 jit_solution(13414141096328614270)
XLA Ops:
  0.0 22.7 %shard_map.154 = bf16[16,4096]{1,0:T(8,128)(2,1)S(1)} custom-call(bf16[16,4096]{1,0:T(8,128)(2,1)} %x_h.1, s32[1,4096]{1,0:T(1,128)} %bitcast.5, bf16[16,64,256]{2,1,0:T(8,128)(2,1)} %bitcast.4, f32[16,64,64]{2,1,0:T(8,128)} %t1_h.1, f32[8,64,64]{2,1,0:T(8,128)} %t2_h.1, f32[1,64,64]{2,1,0:T(8,128)} %t3_h.1, s32[16]{0:T(128)} %parent_h.1, ...), custom_call_target="tpu_custom_call" | custom-call | tf_op jit(solution)/shard_map/pallas_call | solution.py:370
  22.7 0.7 %copy.18 = bf16[16,4096]{1,0:T(8,128)(2,1)} copy(bf16[16,4096]{1,0:T(8,128)(2,1)S(1)} %shard_map.154) | data formatting | bytes 262144

commit v4 on v3

--- a/solution.py
+++ b/solution.py
@@ -12,6 +12,7 @@
 BF16 = jnp.bfloat16
 NN = (((1,), (0,)), ((), ()))
 NT = (((1,), (1,)), ((), ()))
+STEP = 8
 
 
 def dot(a, b, dims=NN):
@@ -135,6 +136,14 @@
     for load in loads[:7]:
         load.start()
 
+    for load in loads[7:]:
+        load.start(priority=1)
+    tile_loads = [
+        pltpu.make_async_copy(tiles_h.at[g], tiles_v.at[g], tile_sem.at[g]) for g in range(leaves)
+    ]
+    for load in tile_loads[:half]:
+        load.start(priority=1)
+
     barrier = pltpu.get_barrier_semaphore()
     peers = [left_id, right_id]
     peers += [(b, lax.rem(j + i, nl)) for i in range(1, nl)]
@@ -142,25 +151,8 @@
     for peer in peers:
         pl.semaphore_signal(barrier, inc=1, device_id=peer, device_id_type=MESH)
 
-    for load in loads[:7]:
-        load.wait()
-    for load in loads[7:]:
-        load.start()
-    tile_loads = [
-        pltpu.make_async_copy(tiles_h.at[g], tiles_v.at[g], tile_sem.at[g]) for g in range(leaves)
-    ]
-    for load in tile_loads:
-        load.start()
-
-    own = [jnp.bitwise_and(parent_s[g], count - 1) for g in range(leaves)]
-    t3_parts = halves(t3_v[0])
-    t2_parts = halves(t2_v[...].reshape(count * rank, rank))
-    lift = (
-        dot(t2_parts[0], t3_parts[0]) + dot(t2_parts[1], t3_parts[0]) + dot(t2_parts[0], t3_parts[1])
-    )
-    for c in range(count):
-        lift_v[c] = stacked(lift[c * rank : (c + 1) * rank])
-
+    loads[0].wait()
+    loads[1].wait()
     order = order_v[...]
     low = jnp.bitwise_and(order, size - 1)
     high = jnp.bitwise_and(jnp.right_shift(order, size.bit_length() - 1), leaves - 1)
@@ -170,8 +162,6 @@
     blocks = jnp.concatenate([x_all[:, h * size : (h + 1) * size] for h in range(leaves)], axis=0)
     spot = lax.broadcasted_iota(jnp.int16, (size, size), 0)
     one, zero = jnp.bfloat16(1), jnp.bfloat16(0)
-    coefs = []
-    raised = jnp.zeros((rows, rank), F32)
     for g in range(leaves):
         cols = slice(g * size, (g + 1) * size)
         onehot = jnp.where(spot == low_short[:, cols], one, zero)
@@ -180,15 +170,34 @@
         chosen = jnp.zeros((rows, size), F32)
         for h in range(leaves):
             chosen = jnp.where(high[:, cols] == h, spread[h * rows : (h + 1) * rows], chosen)
-        chosen = chosen.astype(BF16)
-        window[half + g] = chosen
-        coefs.append(split(dot(chosen, basis_v[g], NT)))
-        direct = times(split(t1_v[g]), lift_v[own[g]])
-        raise_v[g] = direct
-        raised = raised + times(coefs[g], stacked(direct))
+        window[half + g] = chosen.astype(BF16)
+
+    for load in loads[2:7]:
+        load.wait()
+    own = [jnp.bitwise_and(parent_s[g], count - 1) for g in range(leaves)]
+    coefs = [dot(window[half + g], basis_v[g], NT) for g in range(leaves)]
+    t3_parts = halves(t3_v[0])
+    t2_parts = halves(t2_v[...].reshape(count * rank, rank))
+    lift = (
+        dot(t2_parts[0], t3_parts[0]) + dot(t2_parts[1], t3_parts[0]) + dot(t2_parts[0], t3_parts[1])
+    )
+    for c in range(count):
+        lift_v[c] = stacked(lift[c * rank : (c + 1) * rank])
+    coefs = [split(coef) for coef in coefs]
+    for g in range(leaves):
+        raise_v[g] = times(split(t1_v[g]), lift_v[own[g]])
+    wide = []
+    for g in range(leaves):
+        wide += [coefs[g], coefs[g]]
+    raised = dot(
+        jnp.concatenate(wide, axis=1),
+        jnp.concatenate([stacked(raise_v[g]) for g in range(leaves)], axis=0),
+    )
     window[2 * leaves] = jnp.zeros((rows, size), BF16)
     raises[j] = jnp.concatenate([raised, jnp.zeros_like(raised)], axis=1)
 
+    for load in tile_loads[half:]:
+        load.start(priority=1)
     pl.semaphore_wait(barrier, len(peers))
     copies = []
 
@@ -219,19 +228,23 @@
     send(window, leaves, 0, half, x_send.at[0], x_recv.at[0], right_id)
     send(window, half, half + leaves, half, x_send.at[1], x_recv.at[1], left_id)
 
+    moved = [times(coefs[g], stacked(t1_v[g])) for g in range(leaves)]
     parts = [jnp.zeros((rows, rank), F32) for _ in range(count)]
     for g in range(leaves):
-        moved = times(coefs[g], stacked(t1_v[g]))
         for c in range(count):
-            parts[c] = parts[c] + jnp.where(own[g] == c, moved, 0.0)
+            parts[c] = parts[c] + jnp.where(own[g] == c, moved[g], 0.0)
     parts = [split(part) for part in parts]
     for c in range(count):
         clusters[count + c] = parts[c]
     send(clusters, count, 0, count, c_send.at[0], c_recv.at[0], right_id)
     send(clusters, count, 2 * count, count, c_send.at[1], c_recv.at[1], left_id)
-    root = times(parts[0], stacked(t2_v[0]))
-    for c in range(1, count):
-        root = root + times(parts[c], stacked(t2_v[c]))
+    wide = []
+    for c in range(count):
+        wide += [parts[c], parts[c]]
+    root = dot(
+        jnp.concatenate(wide, axis=1),
+        jnp.concatenate([stacked(t2_v[c]) for c in range(count)], axis=0),
+    )
     group[j] = split(root)
     for i in range(1, nl):
         send(group, j, j, 1, g_send.at[i], g_recv.at[j], (b, lax.rem(j + i, nl)))
@@ -267,33 +280,35 @@
     field = jnp.zeros((rows, rank), F32)
     for i in range(nl):
         field = field + mask2_s[0, i].astype(F32) * times(group[i], stacked(c2_v[0, i]))
-    field = split(field)
+    cross = []
     for c in range(count):
-        part = times(field, stacked(t2_v[c].T))
+        part = jnp.zeros((rows, rank), F32)
         for s in range(far):
             at = jnp.bitwise_and(far_s[s, c] - (d - 1) * count, total * count - 1)
             part = part + times(clusters[jnp.minimum(at, 3 * count - 1)], stacked(c1_v[c, s]))
-        field_v[c] = split(part)
+        cross.append(part)
+    field = split(field)
+    cross = [cross[c] + times(field, stacked(t2_v[c].T)) for c in range(count)]
+    for c in range(count):
+        field_v[c] = split(cross[c])
+    inner = [times(field_v[own[g]], stacked(t1_v[g].T)) for g in range(leaves)]
     for g in range(leaves // 2):
         pre_v[:, 2 * g * rank : 2 * (g + 1) * rank] = jnp.concatenate(
-            [
-                times(field_v[own[2 * g + k]], stacked(t1_v[2 * g + k].T))
-                for k in range(2)
-            ],
-            axis=1,
+            inner[2 * g : 2 * g + 2], axis=1
         )
 
     arrive(window, 0, half, x_recv.at[0])
     arrive(window, half + leaves, half, x_recv.at[1])
-    for load in tile_loads:
-        load.wait()
-    for g in range(leaves):
-        picked = []
-        for s in range(slots):
-            at = jnp.bitwise_and(near_s[s, g] - d * leaves + half, total * leaves - 1)
-            at = jnp.where(s < count_s[g], at, 2 * leaves)
-            picked.append(window[jnp.minimum(at, 2 * leaves)])
-        near_v[g] = dot(jnp.concatenate(picked, axis=1), tiles_v[g].reshape(slots * size, size))
+    for first in range(0, leaves, STEP):
+        for g in range(first, first + STEP):
+            tile_loads[g].wait()
+        for g in range(first, first + STEP):
+            picked = []
+            for s in range(slots):
+                at = jnp.bitwise_and(near_s[s, g] - d * leaves + half, total * leaves - 1)
+                at = jnp.where(s < count_s[g], at, 2 * leaves)
+                picked.append(window[jnp.minimum(at, 2 * leaves)])
+            near_v[g] = dot(jnp.concatenate(picked, axis=1), tiles_v[g].reshape(slots * size, size))
 
     for i in range(1, nb):
         src = lax.rem(b + i, nb)
@@ -304,17 +319,19 @@
     top = split(dot(jnp.concatenate(wide, axis=1), c3p_v[...]))
     leaf = (pre_v[...] + times(top, drop_v[...])).astype(BF16)
     lane = lax.broadcasted_iota(jnp.int32, (rows, 2 * rank), 1)
-    product = jnp.zeros((leaves * rows, size), F32)
+    points = []
     for g in range(leaves // 2):
         pair = leaf[:, 2 * g * rank : 2 * (g + 1) * rank].astype(F32)
         both = jnp.concatenate(
             [jnp.where(lane < rank, pair, 0.0), jnp.where(lane < rank, 0.0, pair)], axis=0
         ).astype(BF16)
-        points = dot(both, basis_v[pl.ds(2 * g, 2)].reshape(2 * rank, size))
-        for k in range(2):
-            leaf_out = (points[k * rows : (k + 1) * rows] + near_v[2 * g + k]).astype(BF16)
-            spread = jnp.concatenate([leaf_out] * leaves, axis=0) * place_v[2 * g + k]
-            product = product + dot(spread, pick_v[2 * g + k], NT)
+        points.append(dot(both, basis_v[pl.ds(2 * g, 2)].reshape(2 * rank, size)))
+    product = jnp.zeros((leaves * rows, size), F32)
+    for g in range(leaves):
+        far_out = points[g // 2][g % 2 * rows : (g % 2 + 1) * rows]
+        leaf_out = (far_out + near_v[g]).astype(BF16)
+        spread = jnp.concatenate([leaf_out] * leaves, axis=0) * place_v[g]
+        product = product + dot(spread, pick_v[g], NT)
     for h in range(leaves):
         out_h[:, h * size : (h + 1) * size] = product[h * rows : (h + 1) * rows].astype(BF16)
     for copy in copies:

time: 23.5 us -> 20.8 us (0.89)
  Pallas kernels: 22.7 us -> 20 us
    pallas_call x1, Pallas kernels: 22.7 us -> 20 us  [body(): pl.pallas_call(functools.partial(kernel, nb, nl), out_shape=pltpu.VMEM(po...]
where the time goes in v4:
time: 20.8 us; the launch traced here: 20.7 us
  Pallas kernels  20 us (96%)
  local copies, waits for them, and re-layouts  0.66 us (3%)
    pallas_call x1, Pallas kernels, body(): pl.pallas_call(functools.partial(kernel, nb, nl), out_shape=pltpu.VMEM(po...  20 us
    unnamed x1, local copies, waits for them, and re-layouts  0.66 us

profile of v4, /device:TPU:1, one launch (start us, length us, event | category | flops | bytes accessed | tf_op | source)
XLA Modules:
  0.0 20.7 jit_solution(13094541396572486066)
XLA Ops:
  0.0 20.0 %shard_map.154 = bf16[16,4096]{1,0:T(8,128)(2,1)S(1)} custom-call(bf16[16,4096]{1,0:T(8,128)(2,1)} %x_h.1, s32[1,4096]{1,0:T(1,128)} %bitcast.5, bf16[16,64,256]{2,1,0:T(8,128)(2,1)} %bitcast.4, f32[16,64,64]{2,1,0:T(8,128)} %t1_h.1, f32[8,64,64]{2,1,0:T(8,128)} %t2_h.1, f32[1,64,64]{2,1,0:T(8,128)} %t3_h.1, s32[16]{0:T(128)} %parent_h.1, ...), custom_call_target="tpu_custom_call" | custom-call | tf_op jit(solution)/shard_map/pallas_call | solution.py:387
  20.0 0.7 %copy.18 = bf16[16,4096]{1,0:T(8,128)(2,1)} copy(bf16[16,4096]{1,0:T(8,128)(2,1)S(1)} %shard_map.154) | data formatting | bytes 262144

commit v5 on v4

--- a/solution.py
+++ b/solution.py
@@ -1,4 +1,5 @@
 import functools
+import math
 
 import jax
 import jax.numpy as jnp
@@ -145,9 +146,22 @@
         load.start(priority=1)
 
     barrier = pltpu.get_barrier_semaphore()
-    peers = [left_id, right_id]
-    peers += [(b, lax.rem(j + i, nl)) for i in range(1, nl)]
-    peers += [(lax.rem(b + i, nb), j) for i in range(1, nb)]
+    side = math.isqrt(nb)
+    y, z = b // side, lax.rem(b, side)
+
+    def hops(i, n):
+        return min(i, n - i)
+
+    mates = [
+        lax.rem(j + i, nl) for i in sorted(range(1, nl), key=lambda i: hops(i, nl), reverse=True)
+    ]
+    steps = sorted(
+        [(u, v) for u in range(side) for v in range(side) if u or v],
+        key=lambda uv: hops(uv[0], side) + hops(uv[1], side),
+        reverse=True,
+    )
+    others = [lax.rem(y + u, side) * side + lax.rem(z + v, side) for u, v in steps]
+    peers = [left_id, right_id] + [(b, mate) for mate in mates] + [(other, j) for other in others]
     for peer in peers:
         pl.semaphore_signal(barrier, inc=1, device_id=peer, device_id_type=MESH)
 
@@ -157,35 +171,43 @@
     low = jnp.bitwise_and(order, size - 1)
     high = jnp.bitwise_and(jnp.right_shift(order, size.bit_length() - 1), leaves - 1)
     low_short = low.astype(jnp.int16)
-    high_short = high.astype(jnp.int16)
     x_all = x_v[...]
     blocks = jnp.concatenate([x_all[:, h * size : (h + 1) * size] for h in range(leaves)], axis=0)
     spot = lax.broadcasted_iota(jnp.int16, (size, size), 0)
     one, zero = jnp.bfloat16(1), jnp.bfloat16(0)
-    for g in range(leaves):
-        cols = slice(g * size, (g + 1) * size)
-        onehot = jnp.where(spot == low_short[:, cols], one, zero)
-        pick_v[g] = onehot
+
+    def choose(blocks, onehot, high):
         spread = dot(blocks, onehot)
         chosen = jnp.zeros((rows, size), F32)
         for h in range(leaves):
-            chosen = jnp.where(high[:, cols] == h, spread[h * rows : (h + 1) * rows], chosen)
-        window[half + g] = chosen.astype(BF16)
+            chosen = jnp.where(high == h, spread[h * rows : (h + 1) * rows], chosen)
+        return chosen.astype(BF16)
+
+    def gather(first, last):
+        for g in range(first, last):
+            cols = slice(g * size, (g + 1) * size)
+            onehot = jnp.where(spot == low_short[:, cols], one, zero)
+            pick_v[g] = onehot
+            window[half + g] = choose(blocks, onehot, high[:, cols])
+
+    gather(0, half)
 
     for load in loads[2:7]:
         load.wait()
     own = [jnp.bitwise_and(parent_s[g], count - 1) for g in range(leaves)]
-    coefs = [dot(window[half + g], basis_v[g], NT) for g in range(leaves)]
     t3_parts = halves(t3_v[0])
     t2_parts = halves(t2_v[...].reshape(count * rank, rank))
     lift = (
         dot(t2_parts[0], t3_parts[0]) + dot(t2_parts[1], t3_parts[0]) + dot(t2_parts[0], t3_parts[1])
     )
+    gather(half, leaves - 4)
     for c in range(count):
         lift_v[c] = stacked(lift[c * rank : (c + 1) * rank])
-    coefs = [split(coef) for coef in coefs]
     for g in range(leaves):
         raise_v[g] = times(split(t1_v[g]), lift_v[own[g]])
+    gather(leaves - 4, leaves)
+    coefs = [dot(window[half + g], basis_v[g], NT) for g in range(leaves)]
+    coefs = [split(coef) for coef in coefs]
     wide = []
     for g in range(leaves):
         wide += [coefs[g], coefs[g]]
@@ -223,8 +245,8 @@
             device_id_type=MESH,
         ).wait_recv()
 
-    for i in range(1, nl):
-        send(raises, j, j, 1, s_send.at[i], s_recv.at[j], (b, lax.rem(j + i, nl)))
+    for i, mate in enumerate(mates):
+        send(raises, j, j, 1, s_send.at[i], s_recv.at[j], (b, mate))
     send(window, leaves, 0, half, x_send.at[0], x_recv.at[0], right_id)
     send(window, half, half + leaves, half, x_send.at[1], x_recv.at[1], left_id)
 
@@ -246,25 +268,24 @@
         jnp.concatenate([stacked(t2_v[c]) for c in range(count)], axis=0),
     )
     group[j] = split(root)
-    for i in range(1, nl):
-        send(group, j, j, 1, g_send.at[i], g_recv.at[j], (b, lax.rem(j + i, nl)))
-
-    for i in range(1, nl):
-        src = lax.rem(j + i, nl)
-        arrive(raises, src, 1, s_recv.at[src])
-    subtree = raises[0]
-    for i in range(1, nl):
-        subtree = subtree + raises[i]
-    roots[b] = split(subtree[:, :rank])
-    for i in range(1, nb):
-        send(roots, b, b, 1, r_send.at[i], r_recv.at[b], (lax.rem(b + i, nb), j))
-
+    for i, mate in enumerate(mates):
+        send(group, j, j, 1, g_send.at[i], g_recv.at[j], (b, mate))
+
+    spot_leaf = lax.broadcasted_iota(jnp.int32, (leaves, size), 0)
+    here = lax.broadcasted_iota(jnp.int32, (leaves, size), 1).astype(F32)
+    source = jnp.zeros((2 * leaves, size), F32)
+    for g in range(leaves):
+        match = spot_leaf == high[:, g * size : (g + 1) * size]
+        values = jnp.concatenate(
+            [jnp.where(match, here, 0.0), jnp.where(match, float(g), 0.0)], axis=0
+        ).astype(BF16)
+        source = source + dot(values, pick_v[g], NT)
+    source_low = source[:leaves].astype(jnp.int32).astype(jnp.int16)
+    source_high = source[leaves:].astype(jnp.int32)
+    for h in range(leaves):
+        place_v[h] = jnp.where(spot == source_low[h : h + 1], one, zero)
     for load in loads[7:]:
         load.wait()
-    spot_high = jnp.right_shift(spot, rows.bit_length() - 1)
-    for g in range(leaves):
-        cols = slice(g * size, (g + 1) * size)
-        place_v[g] = jnp.where(spot_high == high_short[:, cols], one, zero)
     for i in range(nb):
         weight = c3_v[0, i] * mask3_s[0, i].astype(F32)
         c3p_v[pl.ds(i * 4 * rank, 4 * rank)] = stacked(weight)
@@ -272,9 +293,18 @@
         drop_v[:, 2 * g * rank : 2 * (g + 1) * rank] = jnp.concatenate(
             [stacked(raise_v[2 * g].T), stacked(raise_v[2 * g + 1].T)], axis=1
         )
+
+    for mate in mates:
+        arrive(raises, mate, 1, s_recv.at[mate])
+    subtree = raises[0]
     for i in range(1, nl):
-        src = lax.rem(j + i, nl)
-        arrive(group, src, 1, g_recv.at[src])
+        subtree = subtree + raises[i]
+    roots[b] = split(subtree[:, :rank])
+    for i, other in enumerate(others):
+        send(roots, b, b, 1, r_send.at[i], r_recv.at[b], (other, j))
+
+    for mate in mates:
+        arrive(group, mate, 1, g_recv.at[mate])
     arrive(clusters, 0, count, c_recv.at[0])
     arrive(clusters, 2 * count, count, c_recv.at[1])
     field = jnp.zeros((rows, rank), F32)
@@ -310,9 +340,8 @@
                 picked.append(window[jnp.minimum(at, 2 * leaves)])
             near_v[g] = dot(jnp.concatenate(picked, axis=1), tiles_v[g].reshape(slots * size, size))
 
-    for i in range(1, nb):
-        src = lax.rem(b + i, nb)
-        arrive(roots, src, 1, r_recv.at[src])
+    for other in others:
+        arrive(roots, other, 1, r_recv.at[other])
     wide = []
     for i in range(nb):
         wide += [roots[i], roots[i]]
@@ -326,14 +355,13 @@
             [jnp.where(lane < rank, pair, 0.0), jnp.where(lane < rank, 0.0, pair)], axis=0
         ).astype(BF16)
         points.append(dot(both, basis_v[pl.ds(2 * g, 2)].reshape(2 * rank, size)))
-    product = jnp.zeros((leaves * rows, size), F32)
+    outs = []
     for g in range(leaves):
         far_out = points[g // 2][g % 2 * rows : (g % 2 + 1) * rows]
-        leaf_out = (far_out + near_v[g]).astype(BF16)
-        spread = jnp.concatenate([leaf_out] * leaves, axis=0) * place_v[g]
-        product = product + dot(spread, pick_v[g], NT)
+        outs.append((far_out + near_v[g]).astype(BF16))
+    blocks = jnp.concatenate(outs, axis=0)
     for h in range(leaves):
-        out_h[:, h * size : (h + 1) * size] = product[h * rows : (h + 1) * rows].astype(BF16)
+        out_h[:, h * size : (h + 1) * size] = choose(blocks, place_v[h], source_high[h : h + 1])
     for copy in copies:
         copy.wait_send()
 

time: 20.8 us -> 20.6 us (level)
    pallas_call x1, Pallas kernels: 20 us -> 19.8 us  [body(): pl.pallas_call(functools.partial(kernel, nb, nl), out_shape=pltpu.VMEM(po...]
where the time goes in v5:
time: 20.6 us; the launch traced here: 20.4 us
  Pallas kernels  19.8 us (96%)
  local copies, waits for them, and re-layouts  0.66 us (3%)
    pallas_call x1, Pallas kernels, body(): pl.pallas_call(functools.partial(kernel, nb, nl), out_shape=pltpu.VMEM(po...  19.8 us
    unnamed x1, local copies, waits for them, and re-layouts  0.66 us

profile of v5, /device:TPU:1, one launch (start us, length us, event | category | flops | bytes accessed | tf_op | source)
XLA Modules:
  0.0 20.4 jit_solution(12158159164904047262)
XLA Ops:
  0.0 19.8 %shard_map.154 = bf16[16,4096]{1,0:T(8,128)(2,1)S(1)} custom-call(bf16[16,4096]{1,0:T(8,128)(2,1)} %x_h.1, s32[1,4096]{1,0:T(1,128)} %bitcast.5, bf16[16,64,256]{2,1,0:T(8,128)(2,1)} %bitcast.4, f32[16,64,64]{2,1,0:T(8,128)} %t1_h.1, f32[8,64,64]{2,1,0:T(8,128)} %t2_h.1, f32[1,64,64]{2,1,0:T(8,128)} %t3_h.1, s32[16]{0:T(128)} %parent_h.1, ...), custom_call_target="tpu_custom_call" | custom-call | tf_op jit(solution)/shard_map/pallas_call | solution.py:415
  19.8 0.7 %copy.18 = bf16[16,4096]{1,0:T(8,128)(2,1)} copy(bf16[16,4096]{1,0:T(8,128)(2,1)S(1)} %shard_map.154) | data formatting | bytes 262144

commit v6 on v5

--- a/solution.py
+++ b/solution.py
@@ -100,6 +100,7 @@
     g_recv,
     r_send,
     r_recv,
+    answer,
 ):
     leaves, rank, size = basis_v.shape
     slots = tiles_v.shape[1]
@@ -134,18 +135,9 @@
         (mask3_h, mask3_s),
     ]
     loads = [pltpu.make_async_copy(src, dst, in_sem.at[i]) for i, (src, dst) in enumerate(pairs)]
-    for load in loads[:7]:
+    for load in loads[:2]:
         load.start()
 
-    for load in loads[7:]:
-        load.start(priority=1)
-    tile_loads = [
-        pltpu.make_async_copy(tiles_h.at[g], tiles_v.at[g], tile_sem.at[g]) for g in range(leaves)
-    ]
-    for load in tile_loads[:half]:
-        load.start(priority=1)
-
-    barrier = pltpu.get_barrier_semaphore()
     side = math.isqrt(nb)
     y, z = b // side, lax.rem(b, side)
 
@@ -161,9 +153,41 @@
         reverse=True,
     )
     others = [lax.rem(y + u, side) * side + lax.rem(z + v, side) for u, v in steps]
-    peers = [left_id, right_id] + [(b, mate) for mate in mates] + [(other, j) for other in others]
-    for peer in peers:
-        pl.semaphore_signal(barrier, inc=1, device_id=peer, device_id_type=MESH)
+
+    barrier = pltpu.get_barrier_semaphore()
+
+    def signal(semaphore, device):
+        pl.semaphore_signal(semaphore, inc=1, device_id=device, device_id_type=MESH)
+
+    def signal_branches(first, last, semaphore):
+        def step(i, carry):
+            signal(semaphore, (i, j))
+            return carry
+
+        lax.fori_loop(first, last, step, 0)
+
+    is_first, is_last = d == 0, d == total - 1
+    for mate in mates:
+        signal(barrier, (b, mate))
+    signal_branches(b + 1, nb, barrier)
+
+    @pl.when(jnp.logical_not(is_last))
+    def _():
+        signal(barrier, right_id)
+
+    @pl.when(is_first)
+    def _():
+        signal(barrier, left_id)
+
+    for load in loads[2:7]:
+        load.start()
+    for load in loads[7:]:
+        load.start(priority=1)
+    tile_loads = [
+        pltpu.make_async_copy(tiles_h.at[g], tiles_v.at[g], tile_sem.at[g]) for g in range(leaves)
+    ]
+    for load in tile_loads[:half]:
+        load.start(priority=1)
 
     loads[0].wait()
     loads[1].wait()
@@ -218,9 +242,8 @@
     window[2 * leaves] = jnp.zeros((rows, size), BF16)
     raises[j] = jnp.concatenate([raised, jnp.zeros_like(raised)], axis=1)
 
-    for load in tile_loads[half:]:
-        load.start(priority=1)
-    pl.semaphore_wait(barrier, len(peers))
+    before = nl - 1 + b + jnp.where(is_first, 0, 1) + jnp.where(is_last, 1, 0)
+    pl.semaphore_wait(barrier, before)
     copies = []
 
     def send(buffer, at, to, count_, send_sem, recv_sem, device):
@@ -247,8 +270,18 @@
 
     for i, mate in enumerate(mates):
         send(raises, j, j, 1, s_send.at[i], s_recv.at[j], (b, mate))
-    send(window, leaves, 0, half, x_send.at[0], x_recv.at[0], right_id)
-    send(window, half, half + leaves, half, x_send.at[1], x_recv.at[1], left_id)
+    signal_branches(0, b, answer)
+
+    @pl.when(jnp.logical_not(is_first))
+    def _():
+        signal(answer, left_id)
+
+    @pl.when(is_last)
+    def _():
+        signal(answer, right_id)
+
+    for load in tile_loads[half:]:
+        load.start(priority=1)
 
     moved = [times(coefs[g], stacked(t1_v[g])) for g in range(leaves)]
     parts = [jnp.zeros((rows, rank), F32) for _ in range(count)]
@@ -258,8 +291,6 @@
     parts = [split(part) for part in parts]
     for c in range(count):
         clusters[count + c] = parts[c]
-    send(clusters, count, 0, count, c_send.at[0], c_recv.at[0], right_id)
-    send(clusters, count, 2 * count, count, c_send.at[1], c_recv.at[1], left_id)
     wide = []
     for c in range(count):
         wide += [parts[c], parts[c]]
@@ -270,6 +301,16 @@
     group[j] = split(root)
     for i, mate in enumerate(mates):
         send(group, j, j, 1, g_send.at[i], g_recv.at[j], (b, mate))
+    behind = nb - 1 - b + jnp.where(is_last, 0, 1) + jnp.where(is_first, 1, 0)
+
+    @pl.when(behind > 0)
+    def _():
+        pl.semaphore_wait(answer, behind)
+
+    send(window, leaves, 0, half, x_send.at[0], x_recv.at[0], right_id)
+    send(window, half, half + leaves, half, x_send.at[1], x_recv.at[1], left_id)
+    send(clusters, count, 0, count, c_send.at[0], c_recv.at[0], right_id)
+    send(clusters, count, 2 * count, count, c_send.at[1], c_recv.at[1], left_id)
 
     spot_leaf = lax.broadcasted_iota(jnp.int32, (leaves, size), 0)
     here = lax.broadcasted_iota(jnp.int32, (leaves, size), 1).astype(F32)
@@ -445,6 +486,7 @@
             dma((nl,)),
             dma((nb,)),
             dma((nb,)),
+            pltpu.SemaphoreType.REGULAR,
         ],
         compiler_params=pltpu.CompilerParams(
             collective_id=0, has_side_effects=True, vmem_limit_bytes=56 * 2**20

time: 20.6 us -> 21.3 us (1.034); the launches traced: 20.4 us -> 20.9 us
  Pallas kernels: 19.8 us -> 20.2 us
    pallas_call x1, Pallas kernels: 19.8 us -> 20.2 us  [body(): pl.pallas_call(functools.partial(kernel, nb, nl), out_shape=pltpu.VMEM(po...]
where the time goes in v6:
time: 21.3 us; the launch traced here: 20.9 us
  Pallas kernels  20.2 us (95%)
  local copies, waits for them, and re-layouts  0.66 us (3%)
    pallas_call x1, Pallas kernels, body(): pl.pallas_call(functools.partial(kernel, nb, nl), out_shape=pltpu.VMEM(po...  20.2 us
    unnamed x1, local copies, waits for them, and re-layouts  0.66 us

profile of v6, /device:TPU:1, one launch (start us, length us, event | category | flops | bytes accessed | tf_op | source)
XLA Modules:
  0.0 20.9 jit_solution(6767808038920247943)
XLA Ops:
  0.0 20.2 %shard_map.154 = bf16[16,4096]{1,0:T(8,128)(2,1)S(1)} custom-call(bf16[16,4096]{1,0:T(8,128)(2,1)} %x_h.1, s32[1,4096]{1,0:T(1,128)} %bitcast.5, bf16[16,64,256]{2,1,0:T(8,128)(2,1)} %bitcast.4, f32[16,64,64]{2,1,0:T(8,128)} %t1_h.1, f32[8,64,64]{2,1,0:T(8,128)} %t2_h.1, f32[1,64,64]{2,1,0:T(8,128)} %t3_h.1, s32[16]{0:T(128)} %parent_h.1, ...), custom_call_target="tpu_custom_call" | custom-call | tf_op jit(solution)/shard_map/pallas_call | solution.py:456
  20.2 0.7 %copy.18 = bf16[16,4096]{1,0:T(8,128)(2,1)} copy(bf16[16,4096]{1,0:T(8,128)(2,1)S(1)} %shard_map.154) | data formatting | bytes 262144

commit v7 on v6

--- a/solution.py
+++ b/solution.py
@@ -159,19 +159,21 @@
     def signal(semaphore, device):
         pl.semaphore_signal(semaphore, inc=1, device_id=device, device_id_type=MESH)
 
-    def signal_branches(first, last, semaphore):
+    def branches(first, last, act):
         def step(i, carry):
-            signal(semaphore, (i, j))
+            act(i)
             return carry
 
         lax.fori_loop(first, last, step, 0)
 
     is_first, is_last = d == 0, d == total - 1
+    after_left = jnp.logical_and(j == 0, jnp.logical_not(is_first))
+    before_right = jnp.logical_and(j == nl - 1, jnp.logical_not(is_last))
     for mate in mates:
         signal(barrier, (b, mate))
-    signal_branches(b + 1, nb, barrier)
-
-    @pl.when(jnp.logical_not(is_last))
+    branches(b + 1, nb, lambda i: signal(barrier, (i, j)))
+
+    @pl.when(before_right)
     def _():
         signal(barrier, right_id)
 
@@ -242,12 +244,12 @@
     window[2 * leaves] = jnp.zeros((rows, size), BF16)
     raises[j] = jnp.concatenate([raised, jnp.zeros_like(raised)], axis=1)
 
-    before = nl - 1 + b + jnp.where(is_first, 0, 1) + jnp.where(is_last, 1, 0)
+    before = nl - 1 + b + jnp.where(after_left, 1, 0) + jnp.where(is_last, 1, 0)
     pl.semaphore_wait(barrier, before)
     copies = []
 
-    def send(buffer, at, to, count_, send_sem, recv_sem, device):
-        copy = pltpu.make_async_remote_copy(
+    def remote(buffer, at, to, count_, send_sem, recv_sem, device):
+        return pltpu.make_async_remote_copy(
             src_ref=buffer.at[pl.ds(at, count_)],
             dst_ref=buffer.at[pl.ds(to, count_)],
             send_sem=send_sem,
@@ -255,8 +257,10 @@
             device_id=device,
             device_id_type=MESH,
         )
-        copy.start()
-        copies.append(copy)
+
+    def send(*args):
+        copies.append(remote(*args))
+        copies[-1].start()
 
     def arrive(buffer, at, count_, recv_sem):
         pltpu.make_async_remote_copy(
@@ -270,15 +274,15 @@
 
     for i, mate in enumerate(mates):
         send(raises, j, j, 1, s_send.at[i], s_recv.at[j], (b, mate))
-    signal_branches(0, b, answer)
-
-    @pl.when(jnp.logical_not(is_first))
-    def _():
-        signal(answer, left_id)
+    branches(0, b, lambda i: signal(answer.at[b], (i, j)))
+
+    @pl.when(after_left)
+    def _():
+        signal(answer.at[nb], left_id)
 
     @pl.when(is_last)
     def _():
-        signal(answer, right_id)
+        signal(answer.at[nb], right_id)
 
     for load in tile_loads[half:]:
         load.start(priority=1)
@@ -301,16 +305,24 @@
     group[j] = split(root)
     for i, mate in enumerate(mates):
         send(group, j, j, 1, g_send.at[i], g_recv.at[j], (b, mate))
-    behind = nb - 1 - b + jnp.where(is_last, 0, 1) + jnp.where(is_first, 1, 0)
-
-    @pl.when(behind > 0)
-    def _():
-        pl.semaphore_wait(answer, behind)
-
-    send(window, leaves, 0, half, x_send.at[0], x_recv.at[0], right_id)
-    send(window, half, half + leaves, half, x_send.at[1], x_recv.at[1], left_id)
-    send(clusters, count, 0, count, c_send.at[0], c_recv.at[0], right_id)
-    send(clusters, count, 2 * count, count, c_send.at[1], c_recv.at[1], left_id)
+    to_right = [
+        remote(window, leaves, 0, half, x_send.at[0], x_recv.at[0], right_id),
+        remote(clusters, count, 0, count, c_send.at[0], c_recv.at[0], right_id),
+    ]
+    to_left = [
+        remote(window, half, half + leaves, half, x_send.at[1], x_recv.at[1], left_id),
+        remote(clusters, count, 2 * count, count, c_send.at[1], c_recv.at[1], left_id),
+    ]
+
+    @pl.when(jnp.logical_not(before_right))
+    def _():
+        for copy in to_right:
+            copy.start()
+
+    @pl.when(jnp.logical_not(is_first))
+    def _():
+        for copy in to_left:
+            copy.start()
 
     spot_leaf = lax.broadcasted_iota(jnp.int32, (leaves, size), 0)
     here = lax.broadcasted_iota(jnp.int32, (leaves, size), 1).astype(F32)
@@ -341,8 +353,28 @@
     for i in range(1, nl):
         subtree = subtree + raises[i]
     roots[b] = split(subtree[:, :rank])
-    for i, other in enumerate(others):
-        send(roots, b, b, 1, r_send.at[i], r_recv.at[b], (other, j))
+
+    def root_to(i):
+        return remote(roots, b, b, 1, r_send.at[i], r_recv.at[b], (i, j))
+
+    def root_behind(i):
+        pl.semaphore_wait(answer.at[i], 1)
+        root_to(i).start()
+
+    branches(0, b, lambda i: root_to(i).start())
+    branches(b + 1, nb, root_behind)
+
+    @pl.when(before_right)
+    def _():
+        pl.semaphore_wait(answer.at[nb], 1)
+        for copy in to_right:
+            copy.start()
+
+    @pl.when(is_first)
+    def _():
+        pl.semaphore_wait(answer.at[nb], 1)
+        for copy in to_left:
+            copy.start()
 
     for mate in mates:
         arrive(group, mate, 1, g_recv.at[mate])
@@ -403,8 +435,10 @@
     blocks = jnp.concatenate(outs, axis=0)
     for h in range(leaves):
         out_h[:, h * size : (h + 1) * size] = choose(blocks, place_v[h], source_high[h : h + 1])
-    for copy in copies:
+    for copy in copies + to_right + to_left:
         copy.wait_send()
+    for other in others:
+        root_to(other).wait_send()
 
 
 def body(
@@ -486,7 +520,7 @@
             dma((nl,)),
             dma((nb,)),
             dma((nb,)),
-            pltpu.SemaphoreType.REGULAR,
+            pltpu.SemaphoreType.REGULAR((nb + 1,)),
         ],
         compiler_params=pltpu.CompilerParams(
             collective_id=0, has_side_effects=True, vmem_limit_bytes=56 * 2**20

time: 21.3 us -> 21.4 us (level)
  the two profiles are of different devices: /device:TPU:1 before, /device:TPU:0 now
where the time goes in v7:
time: 21.4 us; the launch traced here: 21.2 us
  Pallas kernels  20.5 us (96%)
  local copies, waits for them, and re-layouts  0.66 us (3%)
    pallas_call x1, Pallas kernels, body(): pl.pallas_call(functools.partial(kernel, nb, nl), out_shape=pltpu.VMEM(po...  20.5 us
    unnamed x1, local copies, waits for them, and re-layouts  0.66 us

profile of v7, /device:TPU:0, one launch (start us, length us, event | category | flops | bytes accessed | tf_op | source)
XLA Modules:
  0.0 21.2 jit_solution(6528926494619671013)
XLA Ops:
  0.0 20.5 %shard_map.154 = bf16[16,4096]{1,0:T(8,128)(2,1)S(1)} custom-call(bf16[16,4096]{1,0:T(8,128)(2,1)} %x_h.1, s32[1,4096]{1,0:T(1,128)} %bitcast.5, bf16[16,64,256]{2,1,0:T(8,128)(2,1)} %bitcast.4, f32[16,64,64]{2,1,0:T(8,128)} %t1_h.1, f32[8,64,64]{2,1,0:T(8,128)} %t2_h.1, f32[1,64,64]{2,1,0:T(8,128)} %t3_h.1, s32[16]{0:T(128)} %parent_h.1, ...), custom_call_target="tpu_custom_call" | custom-call | tf_op jit(solution)/shard_map/pallas_call | solution.py:490
  20.5 0.7 %copy.18 = bf16[16,4096]{1,0:T(8,128)(2,1)} copy(bf16[16,4096]{1,0:T(8,128)(2,1)S(1)} %shard_map.154) | data formatting | bytes 262144

commit v8 on v7

--- a/solution.py
+++ b/solution.py
@@ -100,6 +100,7 @@
     g_recv,
     r_send,
     r_recv,
+    answers,
     answer,
 ):
     leaves, rank, size = basis_v.shape
@@ -177,7 +178,7 @@
     def _():
         signal(barrier, right_id)
 
-    @pl.when(is_first)
+    @pl.when(j == 0)
     def _():
         signal(barrier, left_id)
 
@@ -190,6 +191,13 @@
     ]
     for load in tile_loads[:half]:
         load.start(priority=1)
+
+    before = nl - 1 + b + jnp.where(after_left, 1, 0) + jnp.where(j == nl - 1, 1, 0)
+
+    @pl.when(is_last)
+    def _():
+        pl.semaphore_wait(barrier, before)
+        signal(answer, right_id)
 
     loads[0].wait()
     loads[1].wait()
@@ -244,8 +252,10 @@
     window[2 * leaves] = jnp.zeros((rows, size), BF16)
     raises[j] = jnp.concatenate([raised, jnp.zeros_like(raised)], axis=1)
 
-    before = nl - 1 + b + jnp.where(after_left, 1, 0) + jnp.where(is_last, 1, 0)
-    pl.semaphore_wait(barrier, before)
+    @pl.when(jnp.logical_not(is_last))
+    def _():
+        pl.semaphore_wait(barrier, before)
+
     copies = []
 
     def remote(buffer, at, to, count_, send_sem, recv_sem, device):
@@ -274,15 +284,7 @@
 
     for i, mate in enumerate(mates):
         send(raises, j, j, 1, s_send.at[i], s_recv.at[j], (b, mate))
-    branches(0, b, lambda i: signal(answer.at[b], (i, j)))
-
-    @pl.when(after_left)
-    def _():
-        signal(answer.at[nb], left_id)
-
-    @pl.when(is_last)
-    def _():
-        signal(answer.at[nb], right_id)
+    branches(0, b, lambda i: signal(answers.at[b], (i, j)))
 
     for load in tile_loads[half:]:
         load.start(priority=1)
@@ -314,10 +316,8 @@
         remote(clusters, count, 2 * count, count, c_send.at[1], c_recv.at[1], left_id),
     ]
 
-    @pl.when(jnp.logical_not(before_right))
-    def _():
-        for copy in to_right:
-            copy.start()
+    for copy in to_right:
+        copy.start()
 
     @pl.when(jnp.logical_not(is_first))
     def _():
@@ -358,23 +358,18 @@
         return remote(roots, b, b, 1, r_send.at[i], r_recv.at[b], (i, j))
 
     def root_behind(i):
-        pl.semaphore_wait(answer.at[i], 1)
+        pl.semaphore_wait(answers.at[i], 1)
         root_to(i).start()
 
     branches(0, b, lambda i: root_to(i).start())
-    branches(b + 1, nb, root_behind)
-
-    @pl.when(before_right)
-    def _():
-        pl.semaphore_wait(answer.at[nb], 1)
-        for copy in to_right:
-            copy.start()
 
     @pl.when(is_first)
     def _():
-        pl.semaphore_wait(answer.at[nb], 1)
+        pl.semaphore_wait(answer, 1)
         for copy in to_left:
             copy.start()
+
+    branches(b + 1, nb, root_behind)
 
     for mate in mates:
         arrive(group, mate, 1, g_recv.at[mate])
@@ -520,7 +515,8 @@
             dma((nl,)),
             dma((nb,)),
             dma((nb,)),
-            pltpu.SemaphoreType.REGULAR((nb + 1,)),
+            pltpu.SemaphoreType.REGULAR((nb,)),
+            pltpu.SemaphoreType.REGULAR,
         ],
         compiler_params=pltpu.CompilerParams(
             collective_id=0, has_side_effects=True, vmem_limit_bytes=56 * 2**20

time: 21.4 us -> 21.7 us (1.014)
  Pallas kernels: 20.5 us -> 20.9 us
    pallas_call x1, Pallas kernels: 20.5 us -> 20.9 us  [body(): pl.pallas_call(functools.partial(kernel, nb, nl), out_shape=pltpu.VMEM(po...]
where the time goes in v8:
time: 21.7 us; the launch traced here: 21.6 us
  Pallas kernels  20.9 us (96%)
  local copies, waits for them, and re-layouts  0.66 us (3%)
    pallas_call x1, Pallas kernels, body(): pl.pallas_call(functools.partial(kernel, nb, nl), out_shape=pltpu.VMEM(po...  20.9 us
    unnamed x1, local copies, waits for them, and re-layouts  0.66 us

profile of v8, /device:TPU:0, one launch (start us, length us, event | category | flops | bytes accessed | tf_op | source)
XLA Modules:
  0.0 21.6 jit_solution(12720193953165335105)
XLA Ops:
  0.0 20.9 %shard_map.154 = bf16[16,4096]{1,0:T(8,128)(2,1)S(1)} custom-call(bf16[16,4096]{1,0:T(8,128)(2,1)} %x_h.1, s32[1,4096]{1,0:T(1,128)} %bitcast.5, bf16[16,64,256]{2,1,0:T(8,128)(2,1)} %bitcast.4, f32[16,64,64]{2,1,0:T(8,128)} %t1_h.1, f32[8,64,64]{2,1,0:T(8,128)} %t2_h.1, f32[1,64,64]{2,1,0:T(8,128)} %t3_h.1, s32[16]{0:T(128)} %parent_h.1, ...), custom_call_target="tpu_custom_call" | custom-call | tf_op jit(solution)/shard_map/pallas_call | solution.py:485
  20.9 0.7 %copy.18 = bf16[16,4096]{1,0:T(8,128)(2,1)} copy(bf16[16,4096]{1,0:T(8,128)(2,1)S(1)} %shard_map.154) | data formatting | bytes 262144

commit v9 on v8

--- a/solution.py
+++ b/solution.py
@@ -13,7 +13,6 @@
 BF16 = jnp.bfloat16
 NN = (((1,), (0,)), ((), ()))
 NT = (((1,), (1,)), ((), ()))
-STEP = 8
 
 
 def dot(a, b, dims=NN):
@@ -284,10 +283,15 @@
 
     for i, mate in enumerate(mates):
         send(raises, j, j, 1, s_send.at[i], s_recv.at[j], (b, mate))
+    to_right = [remote(window, leaves, 0, half, x_send.at[0], x_recv.at[0], right_id)]
+    to_left = [remote(window, half, half + leaves, half, x_send.at[1], x_recv.at[1], left_id)]
+    to_right[0].start()
+
+    @pl.when(jnp.logical_not(is_first))
+    def _():
+        to_left[0].start()
+
     branches(0, b, lambda i: signal(answers.at[b], (i, j)))
-
-    for load in tile_loads[half:]:
-        load.start(priority=1)
 
     moved = [times(coefs[g], stacked(t1_v[g])) for g in range(leaves)]
     parts = [jnp.zeros((rows, rank), F32) for _ in range(count)]
@@ -307,22 +311,15 @@
     group[j] = split(root)
     for i, mate in enumerate(mates):
         send(group, j, j, 1, g_send.at[i], g_recv.at[j], (b, mate))
-    to_right = [
-        remote(window, leaves, 0, half, x_send.at[0], x_recv.at[0], right_id),
-        remote(clusters, count, 0, count, c_send.at[0], c_recv.at[0], right_id),
-    ]
-    to_left = [
-        remote(window, half, half + leaves, half, x_send.at[1], x_recv.at[1], left_id),
-        remote(clusters, count, 2 * count, count, c_send.at[1], c_recv.at[1], left_id),
-    ]
-
-    for copy in to_right:
-        copy.start()
+    to_right.append(remote(clusters, count, 0, count, c_send.at[0], c_recv.at[0], right_id))
+    to_left.append(
+        remote(clusters, count, 2 * count, count, c_send.at[1], c_recv.at[1], left_id)
+    )
+    to_right[1].start()
 
     @pl.when(jnp.logical_not(is_first))
     def _():
-        for copy in to_left:
-            copy.start()
+        to_left[1].start()
 
     spot_leaf = lax.broadcasted_iota(jnp.int32, (leaves, size), 0)
     here = lax.broadcasted_iota(jnp.int32, (leaves, size), 1).astype(F32)
@@ -362,6 +359,8 @@
         root_to(i).start()
 
     branches(0, b, lambda i: root_to(i).start())
+    for load in tile_loads[half:]:
+        load.start(priority=1)
 
     @pl.when(is_first)
     def _():
@@ -370,6 +369,22 @@
             copy.start()
 
     branches(b + 1, nb, root_behind)
+
+    arrive(window, 0, half, x_recv.at[0])
+    arrive(window, half + leaves, half, x_recv.at[1])
+
+    def near(first, last):
+        for g in range(first, last):
+            tile_loads[g].wait()
+        for g in range(first, last):
+            picked = []
+            for s in range(slots):
+                at = jnp.bitwise_and(near_s[s, g] - d * leaves + half, total * leaves - 1)
+                at = jnp.where(s < count_s[g], at, 2 * leaves)
+                picked.append(window[jnp.minimum(at, 2 * leaves)])
+            near_v[g] = dot(jnp.concatenate(picked, axis=1), tiles_v[g].reshape(slots * size, size))
+
+    near(0, half)
 
     for mate in mates:
         arrive(group, mate, 1, g_recv.at[mate])
@@ -395,18 +410,7 @@
             inner[2 * g : 2 * g + 2], axis=1
         )
 
-    arrive(window, 0, half, x_recv.at[0])
-    arrive(window, half + leaves, half, x_recv.at[1])
-    for first in range(0, leaves, STEP):
-        for g in range(first, first + STEP):
-            tile_loads[g].wait()
-        for g in range(first, first + STEP):
-            picked = []
-            for s in range(slots):
-                at = jnp.bitwise_and(near_s[s, g] - d * leaves + half, total * leaves - 1)
-                at = jnp.where(s < count_s[g], at, 2 * leaves)
-                picked.append(window[jnp.minimum(at, 2 * leaves)])
-            near_v[g] = dot(jnp.concatenate(picked, axis=1), tiles_v[g].reshape(slots * size, size))
+    near(half, leaves)
 
     for other in others:
         arrive(roots, other, 1, r_recv.at[other])

time: 21.7 us -> 21.1 us (0.972)
  Pallas kernels: 20.9 us -> 20.3 us
    pallas_call x1, Pallas kernels: 20.9 us -> 20.3 us  [body(): pl.pallas_call(functools.partial(kernel, nb, nl), out_shape=pltpu.VMEM(po...]
where the time goes in v9:
time: 21.1 us; the launch traced here: 21 us
  Pallas kernels  20.3 us (96%)
  local copies, waits for them, and re-layouts  0.66 us (3%)
    pallas_call x1, Pallas kernels, body(): pl.pallas_call(functools.partial(kernel, nb, nl), out_shape=pltpu.VMEM(po...  20.3 us
    unnamed x1, local copies, waits for them, and re-layouts  0.66 us

profile of v9, /device:TPU:0, one launch (start us, length us, event | category | flops | bytes accessed | tf_op | source)
XLA Modules:
  0.0 21.0 jit_solution(16639008470132882084)
XLA Ops:
  0.0 20.3 %shard_map.154 = bf16[16,4096]{1,0:T(8,128)(2,1)S(1)} custom-call(bf16[16,4096]{1,0:T(8,128)(2,1)} %x_h.1, s32[1,4096]{1,0:T(1,128)} %bitcast.5, bf16[16,64,256]{2,1,0:T(8,128)(2,1)} %bitcast.4, f32[16,64,64]{2,1,0:T(8,128)} %t1_h.1, f32[8,64,64]{2,1,0:T(8,128)} %t2_h.1, f32[1,64,64]{2,1,0:T(8,128)} %t3_h.1, s32[16]{0:T(128)} %parent_h.1, ...), custom_call_target="tpu_custom_call" | custom-call | tf_op jit(solution)/shard_map/pallas_call | solution.py:489
  20.3 0.7 %copy.18 = bf16[16,4096]{1,0:T(8,128)(2,1)} copy(bf16[16,4096]{1,0:T(8,128)(2,1)S(1)} %shard_map.154) | data formatting | bytes 262144

commit v10 on v9

--- a/solution.py
+++ b/solution.py
@@ -75,7 +75,8 @@
     tiles_v,
     pick_v,
     place_v,
-    window,
+    lower,
+    upper,
     clusters,
     lift_v,
     raise_v,
@@ -188,8 +189,18 @@
     tile_loads = [
         pltpu.make_async_copy(tiles_h.at[g], tiles_v.at[g], tile_sem.at[g]) for g in range(leaves)
     ]
-    for load in tile_loads[:half]:
+    for load in tile_loads[half:]:
         load.start(priority=1)
+
+    def remote(buffer, at, to, count_, send_sem, recv_sem, device):
+        return pltpu.make_async_remote_copy(
+            src_ref=buffer.at[pl.ds(at, count_)],
+            dst_ref=buffer.at[pl.ds(to, count_)],
+            send_sem=send_sem,
+            recv_sem=recv_sem,
+            device_id=device,
+            device_id_type=MESH,
+        )
 
     before = nl - 1 + b + jnp.where(after_left, 1, 0) + jnp.where(j == nl - 1, 1, 0)
 
@@ -221,7 +232,9 @@
             cols = slice(g * size, (g + 1) * size)
             onehot = jnp.where(spot == low_short[:, cols], one, zero)
             pick_v[g] = onehot
-            window[half + g] = choose(blocks, onehot, high[:, cols])
+            chosen = choose(blocks, onehot, high[:, cols])
+            lower[half + g] = chosen
+            upper[g] = chosen
 
     gather(0, half)
 
@@ -239,7 +252,13 @@
     for g in range(leaves):
         raise_v[g] = times(split(t1_v[g]), lift_v[own[g]])
     gather(leaves - 4, leaves)
-    coefs = [dot(window[half + g], basis_v[g], NT) for g in range(leaves)]
+    to_right = [remote(lower, leaves, 0, half, x_send.at[0], x_recv.at[0], right_id)]
+
+    @pl.when(is_last)
+    def _():
+        to_right[0].start()
+
+    coefs = [dot(upper[g], basis_v[g], NT) for g in range(leaves)]
     coefs = [split(coef) for coef in coefs]
     wide = []
     for g in range(leaves):
@@ -248,7 +267,8 @@
         jnp.concatenate(wide, axis=1),
         jnp.concatenate([stacked(raise_v[g]) for g in range(leaves)], axis=0),
     )
-    window[2 * leaves] = jnp.zeros((rows, size), BF16)
+    lower[leaves + half] = jnp.zeros((rows, size), BF16)
+    upper[leaves + half] = jnp.zeros((rows, size), BF16)
     raises[j] = jnp.concatenate([raised, jnp.zeros_like(raised)], axis=1)
 
     @pl.when(jnp.logical_not(is_last))
@@ -256,16 +276,6 @@
         pl.semaphore_wait(barrier, before)
 
     copies = []
-
-    def remote(buffer, at, to, count_, send_sem, recv_sem, device):
-        return pltpu.make_async_remote_copy(
-            src_ref=buffer.at[pl.ds(at, count_)],
-            dst_ref=buffer.at[pl.ds(to, count_)],
-            send_sem=send_sem,
-            recv_sem=recv_sem,
-            device_id=device,
-            device_id_type=MESH,
-        )
 
     def send(*args):
         copies.append(remote(*args))
@@ -283,9 +293,11 @@
 
     for i, mate in enumerate(mates):
         send(raises, j, j, 1, s_send.at[i], s_recv.at[j], (b, mate))
-    to_right = [remote(window, leaves, 0, half, x_send.at[0], x_recv.at[0], right_id)]
-    to_left = [remote(window, half, half + leaves, half, x_send.at[1], x_recv.at[1], left_id)]
-    to_right[0].start()
+    to_left = [remote(upper, 0, leaves, half, x_send.at[1], x_recv.at[1], left_id)]
+
+    @pl.when(jnp.logical_not(is_last))
+    def _():
+        to_right[0].start()
 
     @pl.when(jnp.logical_not(is_first))
     def _():
@@ -359,7 +371,7 @@
         root_to(i).start()
 
     branches(0, b, lambda i: root_to(i).start())
-    for load in tile_loads[half:]:
+    for load in tile_loads[:half]:
         load.start(priority=1)
 
     @pl.when(is_first)
@@ -370,21 +382,21 @@
 
     branches(b + 1, nb, root_behind)
 
-    arrive(window, 0, half, x_recv.at[0])
-    arrive(window, half + leaves, half, x_recv.at[1])
-
-    def near(first, last):
+    def near(first, last, window, start):
         for g in range(first, last):
             tile_loads[g].wait()
         for g in range(first, last):
             picked = []
             for s in range(slots):
-                at = jnp.bitwise_and(near_s[s, g] - d * leaves + half, total * leaves - 1)
-                at = jnp.where(s < count_s[g], at, 2 * leaves)
-                picked.append(window[jnp.minimum(at, 2 * leaves)])
+                at = jnp.bitwise_and(near_s[s, g] - d * leaves - start, total * leaves - 1)
+                at = jnp.where(s < count_s[g], at, leaves + half)
+                picked.append(window[jnp.minimum(at, leaves + half)])
             near_v[g] = dot(jnp.concatenate(picked, axis=1), tiles_v[g].reshape(slots * size, size))
 
-    near(0, half)
+    arrive(upper, leaves, half, x_recv.at[1])
+    near(half, leaves, upper, 0)
+    arrive(lower, 0, half, x_recv.at[0])
+    near(0, half, lower, -half)
 
     for mate in mates:
         arrive(group, mate, 1, g_recv.at[mate])
@@ -410,9 +422,12 @@
             inner[2 * g : 2 * g + 2], axis=1
         )
 
-    near(half, leaves)
-
+    for copy in copies + to_right + to_left:
+        copy.wait_send()
     for other in others:
+        root_to(other).wait_send()
+    for u, v in sorted(steps, key=sum):
+        other = lax.rem(y + u, side) * side + lax.rem(z + v, side)
         arrive(roots, other, 1, r_recv.at[other])
     wide = []
     for i in range(nb):
@@ -434,10 +449,6 @@
     blocks = jnp.concatenate(outs, axis=0)
     for h in range(leaves):
         out_h[:, h * size : (h + 1) * size] = choose(blocks, place_v[h], source_high[h : h + 1])
-    for copy in copies + to_right + to_left:
-        copy.wait_send()
-    for other in others:
-        root_to(other).wait_send()
 
 
 def body(
@@ -495,7 +506,8 @@
         + [
             pltpu.VMEM((leaves, size, size), BF16),
             pltpu.VMEM((leaves, size, size), BF16),
-            pltpu.VMEM((2 * leaves + 1, rows, size), BF16),
+            pltpu.VMEM((leaves + leaves // 2 + 1, rows, size), BF16),
+            pltpu.VMEM((leaves + leaves // 2 + 1, rows, size), BF16),
             pltpu.VMEM((3 * count, rows, 2 * rank), BF16),
             pltpu.VMEM((count, 4 * rank, rank), BF16),
             pltpu.VMEM((leaves, rank, rank), F32),

time: 21.1 us -> 19.9 us (0.943)
  the two profiles are of different devices: /device:TPU:0 before, /device:TPU:1 now
where the time goes in v10:
time: 19.9 us; the launch traced here: 19.7 us
  Pallas kernels  19.1 us (96%)
  local copies, waits for them, and re-layouts  0.66 us (3%)
    pallas_call x1, Pallas kernels, body(): pl.pallas_call(functools.partial(kernel, nb, nl), out_shape=pltpu.VMEM(po...  19.1 us
    unnamed x1, local copies, waits for them, and re-layouts  0.66 us

profile of v10, /device:TPU:1, one launch (start us, length us, event | category | flops | bytes accessed | tf_op | source)
XLA Modules:
  0.0 19.7 jit_solution(3861443496923378076)
XLA Ops:
  0.0 19.1 %shard_map.154 = bf16[16,4096]{1,0:T(8,128)(2,1)S(1)} custom-call(bf16[16,4096]{1,0:T(8,128)(2,1)} %x_h.1, s32[1,4096]{1,0:T(1,128)} %bitcast.5, bf16[16,64,256]{2,1,0:T(8,128)(2,1)} %bitcast.4, f32[16,64,64]{2,1,0:T(8,128)} %t1_h.1, f32[8,64,64]{2,1,0:T(8,128)} %t2_h.1, f32[1,64,64]{2,1,0:T(8,128)} %t3_h.1, s32[16]{0:T(128)} %parent_h.1, ...), custom_call_target="tpu_custom_call" | custom-call | tf_op jit(solution)/shard_map/pallas_call | solution.py:500
  19.1 0.7 %copy.18 = bf16[16,4096]{1,0:T(8,128)(2,1)} copy(bf16[16,4096]{1,0:T(8,128)(2,1)S(1)} %shard_map.154) | data formatting | bytes 262144

commit v11 on v10

--- a/solution.py
+++ b/solution.py
@@ -160,19 +160,25 @@
     def signal(semaphore, device):
         pl.semaphore_signal(semaphore, inc=1, device_id=device, device_id_type=MESH)
 
-    def branches(first, last, act):
-        def step(i, carry):
-            act(i)
-            return carry
-
-        lax.fori_loop(first, last, step, 0)
+    places = sorted(
+        [(u, v) for u in range(side) for v in range(side)], key=lambda uv: 5 * uv[0] + 9 * uv[1]
+    )
+    place = 5 * y + 9 * z
+
+    def branches(ahead, act):
+        for u, v in places:
+            spot_of = 5 * u + 9 * v
+
+            @pl.when(spot_of < place if ahead else spot_of > place)
+            def _():
+                act(u * side + v)
 
     is_first, is_last = d == 0, d == total - 1
     after_left = jnp.logical_and(j == 0, jnp.logical_not(is_first))
     before_right = jnp.logical_and(j == nl - 1, jnp.logical_not(is_last))
     for mate in mates:
         signal(barrier, (b, mate))
-    branches(b + 1, nb, lambda i: signal(barrier, (i, j)))
+    branches(False, lambda i: signal(barrier, (i, j)))
 
     @pl.when(before_right)
     def _():
@@ -202,7 +208,8 @@
             device_id_type=MESH,
         )
 
-    before = nl - 1 + b + jnp.where(after_left, 1, 0) + jnp.where(j == nl - 1, 1, 0)
+    ahead = sum(jnp.where(5 * u + 9 * v < place, 1, 0) for u, v in places)
+    before = nl - 1 + ahead + jnp.where(after_left, 1, 0) + jnp.where(j == nl - 1, 1, 0)
 
     @pl.when(is_last)
     def _():
@@ -303,7 +310,7 @@
     def _():
         to_left[0].start()
 
-    branches(0, b, lambda i: signal(answers.at[b], (i, j)))
+    branches(True, lambda i: signal(answers.at[b], (i, j)))
 
     moved = [times(coefs[g], stacked(t1_v[g])) for g in range(leaves)]
     parts = [jnp.zeros((rows, rank), F32) for _ in range(count)]
@@ -370,7 +377,7 @@
         pl.semaphore_wait(answers.at[i], 1)
         root_to(i).start()
 
-    branches(0, b, lambda i: root_to(i).start())
+    branches(True, lambda i: root_to(i).start())
     for load in tile_loads[:half]:
         load.start(priority=1)
 
@@ -380,7 +387,7 @@
         for copy in to_left:
             copy.start()
 
-    branches(b + 1, nb, root_behind)
+    branches(False, root_behind)
 
     def near(first, last, window, start):
         for g in range(first, last):

time: 19.9 us -> 19.9 us (level)
  no operation moved by 1% of the time
where the time goes in v11:
time: 19.9 us; the launch traced here: 19.7 us
  Pallas kernels  19.1 us (96%)
  local copies, waits for them, and re-layouts  0.66 us (3%)
    pallas_call x1, Pallas kernels, body(): pl.pallas_call(functools.partial(kernel, nb, nl), out_shape=pltpu.VMEM(po...  19.1 us
    unnamed x1, local copies, waits for them, and re-layouts  0.66 us

profile of v11, /device:TPU:1, one launch (start us, length us, event | category | flops | bytes accessed | tf_op | source)
XLA Modules:
  0.0 19.7 jit_solution(9309618123606153247)
XLA Ops:
  0.0 19.1 %shard_map.154 = bf16[16,4096]{1,0:T(8,128)(2,1)S(1)} custom-call(bf16[16,4096]{1,0:T(8,128)(2,1)} %x_h.1, s32[1,4096]{1,0:T(1,128)} %bitcast.5, bf16[16,64,256]{2,1,0:T(8,128)(2,1)} %bitcast.4, f32[16,64,64]{2,1,0:T(8,128)} %t1_h.1, f32[8,64,64]{2,1,0:T(8,128)} %t2_h.1, f32[1,64,64]{2,1,0:T(8,128)} %t3_h.1, s32[16]{0:T(128)} %parent_h.1, ...), custom_call_target="tpu_custom_call" | custom-call | tf_op jit(solution)/shard_map/pallas_call | solution.py:507
  19.1 0.7 %copy.18 = bf16[16,4096]{1,0:T(8,128)(2,1)} copy(bf16[16,4096]{1,0:T(8,128)(2,1)S(1)} %shard_map.154) | data formatting | bytes 262144

commit v12 on v11

--- a/solution.py
+++ b/solution.py
@@ -178,18 +178,18 @@
     before_right = jnp.logical_and(j == nl - 1, jnp.logical_not(is_last))
     for mate in mates:
         signal(barrier, (b, mate))
-    branches(False, lambda i: signal(barrier, (i, j)))
-
-    @pl.when(before_right)
-    def _():
-        signal(barrier, right_id)
-
-    @pl.when(j == 0)
-    def _():
-        signal(barrier, left_id)
-
     for load in loads[2:7]:
         load.start()
+    branches(False, lambda i: signal(barrier, (i, j)))
+
+    @pl.when(before_right)
+    def _():
+        signal(barrier, right_id)
+
+    @pl.when(j == 0)
+    def _():
+        signal(barrier, left_id)
+
     for load in loads[7:]:
         load.start(priority=1)
     tile_loads = [
@@ -302,14 +302,6 @@
         send(raises, j, j, 1, s_send.at[i], s_recv.at[j], (b, mate))
     to_left = [remote(upper, 0, leaves, half, x_send.at[1], x_recv.at[1], left_id)]
 
-    @pl.when(jnp.logical_not(is_last))
-    def _():
-        to_right[0].start()
-
-    @pl.when(jnp.logical_not(is_first))
-    def _():
-        to_left[0].start()
-
     branches(True, lambda i: signal(answers.at[b], (i, j)))
 
     moved = [times(coefs[g], stacked(t1_v[g])) for g in range(leaves)]
@@ -320,6 +312,12 @@
     parts = [split(part) for part in parts]
     for c in range(count):
         clusters[count + c] = parts[c]
+    to_right.append(remote(clusters, count, 0, count, c_send.at[0], c_recv.at[0], right_id))
+
+    @pl.when(is_last)
+    def _():
+        to_right[1].start()
+
     wide = []
     for c in range(count):
         wide += [parts[c], parts[c]]
@@ -330,15 +328,19 @@
     group[j] = split(root)
     for i, mate in enumerate(mates):
         send(group, j, j, 1, g_send.at[i], g_recv.at[j], (b, mate))
-    to_right.append(remote(clusters, count, 0, count, c_send.at[0], c_recv.at[0], right_id))
     to_left.append(
         remote(clusters, count, 2 * count, count, c_send.at[1], c_recv.at[1], left_id)
     )
-    to_right[1].start()
+
+    @pl.when(jnp.logical_not(is_last))
+    def _():
+        for copy in to_right:
+            copy.start()
 
     @pl.when(jnp.logical_not(is_first))
     def _():
-        to_left[1].start()
+        for copy in to_left:
+            copy.start()
 
     spot_leaf = lax.broadcasted_iota(jnp.int32, (leaves, size), 0)
     here = lax.broadcasted_iota(jnp.int32, (leaves, size), 1).astype(F32)

time: 19.9 us -> 19.9 us (level)
  no operation moved by 1% of the time
where the time goes in v12:
time: 19.9 us; the launch traced here: 19.8 us
  Pallas kernels  19.1 us (96%)
  local copies, waits for them, and re-layouts  0.66 us (3%)
    pallas_call x1, Pallas kernels, body(): pl.pallas_call(functools.partial(kernel, nb, nl), out_shape=pltpu.VMEM(po...  19.1 us
    unnamed x1, local copies, waits for them, and re-layouts  0.66 us

profile of v12, /device:TPU:1, one launch (start us, length us, event | category | flops | bytes accessed | tf_op | source)
XLA Modules:
  0.0 19.8 jit_solution(6204470254775226083)
XLA Ops:
  0.0 19.1 %shard_map.154 = bf16[16,4096]{1,0:T(8,128)(2,1)S(1)} custom-call(bf16[16,4096]{1,0:T(8,128)(2,1)} %x_h.1, s32[1,4096]{1,0:T(1,128)} %bitcast.5, bf16[16,64,256]{2,1,0:T(8,128)(2,1)} %bitcast.4, f32[16,64,64]{2,1,0:T(8,128)} %t1_h.1, f32[8,64,64]{2,1,0:T(8,128)} %t2_h.1, f32[1,64,64]{2,1,0:T(8,128)} %t3_h.1, s32[16]{0:T(128)} %parent_h.1, ...), custom_call_target="tpu_custom_call" | custom-call | tf_op jit(solution)/shard_map/pallas_call | solution.py:509
  19.1 0.7 %copy.18 = bf16[16,4096]{1,0:T(8,128)(2,1)} copy(bf16[16,4096]{1,0:T(8,128)(2,1)S(1)} %shard_map.154) | data formatting | bytes 262144

commit v13 on v12

--- a/solution.py
+++ b/solution.py
@@ -256,8 +256,6 @@
     gather(half, leaves - 4)
     for c in range(count):
         lift_v[c] = stacked(lift[c * rank : (c + 1) * rank])
-    for g in range(leaves):
-        raise_v[g] = times(split(t1_v[g]), lift_v[own[g]])
     gather(leaves - 4, leaves)
     to_right = [remote(lower, leaves, 0, half, x_send.at[0], x_recv.at[0], right_id)]
 
@@ -267,13 +265,17 @@
 
     coefs = [dot(upper[g], basis_v[g], NT) for g in range(leaves)]
     coefs = [split(coef) for coef in coefs]
-    wide = []
+    moved = [times(coefs[g], stacked(t1_v[g])) for g in range(leaves)]
+    parts = [jnp.zeros((rows, rank), F32) for _ in range(count)]
     for g in range(leaves):
-        wide += [coefs[g], coefs[g]]
-    raised = dot(
-        jnp.concatenate(wide, axis=1),
-        jnp.concatenate([stacked(raise_v[g]) for g in range(leaves)], axis=0),
-    )
+        for c in range(count):
+            parts[c] = parts[c] + jnp.where(own[g] == c, moved[g], 0.0)
+    parts = [split(part) for part in parts]
+    doubled = []
+    for part in parts:
+        doubled += [part, part]
+    doubled = jnp.concatenate(doubled, axis=1)
+    raised = dot(doubled, jnp.concatenate([lift_v[c] for c in range(count)], axis=0))
     lower[leaves + half] = jnp.zeros((rows, size), BF16)
     upper[leaves + half] = jnp.zeros((rows, size), BF16)
     raises[j] = jnp.concatenate([raised, jnp.zeros_like(raised)], axis=1)
@@ -304,12 +306,6 @@
 
     branches(True, lambda i: signal(answers.at[b], (i, j)))
 
-    moved = [times(coefs[g], stacked(t1_v[g])) for g in range(leaves)]
-    parts = [jnp.zeros((rows, rank), F32) for _ in range(count)]
-    for g in range(leaves):
-        for c in range(count):
-            parts[c] = parts[c] + jnp.where(own[g] == c, moved[g], 0.0)
-    parts = [split(part) for part in parts]
     for c in range(count):
         clusters[count + c] = parts[c]
     to_right.append(remote(clusters, count, 0, count, c_send.at[0], c_recv.at[0], right_id))
@@ -318,11 +314,8 @@
     def _():
         to_right[1].start()
 
-    wide = []
-    for c in range(count):
-        wide += [parts[c], parts[c]]
     root = dot(
-        jnp.concatenate(wide, axis=1),
+        doubled,
         jnp.concatenate([stacked(t2_v[c]) for c in range(count)], axis=0),
     )
     group[j] = split(root)
@@ -357,13 +350,6 @@
         place_v[h] = jnp.where(spot == source_low[h : h + 1], one, zero)
     for load in loads[7:]:
         load.wait()
-    for i in range(nb):
-        weight = c3_v[0, i] * mask3_s[0, i].astype(F32)
-        c3p_v[pl.ds(i * 4 * rank, 4 * rank)] = stacked(weight)
-    for g in range(leaves // 2):
-        drop_v[:, 2 * g * rank : 2 * (g + 1) * rank] = jnp.concatenate(
-            [stacked(raise_v[2 * g].T), stacked(raise_v[2 * g + 1].T)], axis=1
-        )
 
     for mate in mates:
         arrive(raises, mate, 1, s_recv.at[mate])
@@ -389,7 +375,16 @@
         for copy in to_left:
             copy.start()
 
-    branches(False, root_behind)
+
+    for i in range(nb):
+        weight = c3_v[0, i] * mask3_s[0, i].astype(F32)
+        c3p_v[pl.ds(i * 4 * rank, 4 * rank)] = stacked(weight)
+    for g in range(leaves):
+        raise_v[g] = times(split(t1_v[g]), lift_v[own[g]])
+    for g in range(leaves // 2):
+        drop_v[:, 2 * g * rank : 2 * (g + 1) * rank] = jnp.concatenate(
+            [stacked(raise_v[2 * g].T), stacked(raise_v[2 * g + 1].T)], axis=1
+        )
 
     def near(first, last, window, start):
         for g in range(first, last):
@@ -404,6 +399,7 @@
 
     arrive(upper, leaves, half, x_recv.at[1])
     near(half, leaves, upper, 0)
+    branches(False, root_behind)
     arrive(lower, 0, half, x_recv.at[0])
     near(0, half, lower, -half)
 

time: 19.9 us -> 19.8 us (level)
  no operation moved by 1% of the time
where the time goes in v13:
time: 19.8 us; the launch traced here: 19.6 us
  Pallas kernels  19 us (96%)
  local copies, waits for them, and re-layouts  0.66 us (3%)
    pallas_call x1, Pallas kernels, body(): pl.pallas_call(functools.partial(kernel, nb, nl), out_shape=pltpu.VMEM(po...  19 us
    unnamed x1, local copies, waits for them, and re-layouts  0.66 us

profile of v13, /device:TPU:1, one launch (start us, length us, event | category | flops | bytes accessed | tf_op | source)
XLA Modules:
  0.0 19.6 jit_solution(2527687320735341219)
XLA Ops:
  0.0 19.0 %shard_map.154 = bf16[16,4096]{1,0:T(8,128)(2,1)S(1)} custom-call(bf16[16,4096]{1,0:T(8,128)(2,1)} %x_h.1, s32[1,4096]{1,0:T(1,128)} %bitcast.5, bf16[16,64,256]{2,1,0:T(8,128)(2,1)} %bitcast.4, f32[16,64,64]{2,1,0:T(8,128)} %t1_h.1, f32[8,64,64]{2,1,0:T(8,128)} %t2_h.1, f32[1,64,64]{2,1,0:T(8,128)} %t3_h.1, s32[16]{0:T(128)} %parent_h.1, ...), custom_call_target="tpu_custom_call" | custom-call | tf_op jit(solution)/shard_map/pallas_call | solution.py:505
  19.0 0.7 %copy.18 = bf16[16,4096]{1,0:T(8,128)(2,1)} copy(bf16[16,4096]{1,0:T(8,128)(2,1)S(1)} %shard_map.154) | data formatting | bytes 262144
